TPU v7x, 256 devices: a whole 4x4x8 slice. The times are simulated.
256 devices in a mesh: surf: 32 (over z, y_hi, core), neur: 8 (over x, y_lo).
Axes of the slice: x: 4, y: 4 (y_hi: 2, y_lo: 2; y = y_hi * 2 + y_lo), z: 8, core: 2. Of those that a mesh axis runs over, the one named last changes fastest.
Arguments:
- spike_bins: int32 [16, 64, 32768], P(None, 'neur', 'surf'), may hold values from 0 to 10
- neuron_site: int32 [64, 32768], P('neur', 'surf'), may hold values from 0 to 1023
- efficacy: bfloat16 [64, 32768], P('neur', 'surf'), may hold values from 0.5 to 2
- region_live: int32 [64], P('neur'), may hold values from 1 to 32768, 1258291 in all
- membrane_init: float32 [16, 64, 32768], P(None, 'neur', 'surf'), may hold values from -4 to 4
- field_init: float32 [16, 64, 1024], P(None, 'neur', 'surf'), may hold values from -6 to 6
- rim_weights: float32 [6, 64, 1024], P(None, 'neur', 'surf'), may hold values from 0.2 to 1
- rim_codes: int32 [6, 64, 1024], P(None, 'neur', 'surf'), may hold values from 0 to 24, as said below
Outputs:
- field_final: float32 [16, 64, 1024], P(None, 'neur', 'surf')
- membranes: float32 [16, 64, 32768], P(None, 'neur', 'surf')
Inputs may be any that keep to these rules, and one draw needn't show every extreme that they name: `spike_bins`: a bin of 10 means that the neuron does not spike in the window. `rim_codes`: the codes of one vertex are distinct and never 2 * 6.
All inputs are finite; a program needn't handle non-finite values. No bound on the sum of `region_live` on one device may be relied on, other than what follows from the above.
Results may differ from a plain program's by a relative error of at most 0.006.
Values may be sent and summed in bfloat16 or wider, within the bound.
A program may use at most 256 MiB of HBM per device.

v0:
```python
import jax
import jax.numpy as jnp
from jax import lax
from jax.sharding import PartitionSpec as P

STEPS = 10
RIM = 2
FOOT = 8


def padded(shard, sides, width, wrap):
    for axis, dim in sides:
        count, length = (lax.axis_size(axis), shard.shape[dim])
        up = [(i, (i + 1) % count) for i in range(count if wrap else count - 1)]
        down = [(j, i) for i, j in up]
        last = lax.slice_in_dim(shard, length - width, length, axis=dim)
        leading = lax.slice_in_dim(shard, 0, width, axis=dim)
        before = lax.ppermute(last, axis, up)
        after = lax.ppermute(leading, axis, down)
        shard = jnp.concatenate([before, shard, after], axis=dim)
    return shard


def footprint():
    spread = jnp.exp(-0.5 * jnp.arange(FOOT, dtype=jnp.float32))
    return spread / jnp.sum(spread)


def stencil(rim_weights, rim_codes):
    reach_span = 2 * RIM + 1
    entries = []
    for row_shift in range(-RIM, RIM + 1):
        for col_shift in range(-RIM, RIM + 1):
            if row_shift == 0 and col_shift == 0:
                continue
            code_value = (row_shift + RIM) * reach_span + (col_shift + RIM)
            weight = jnp.sum(
                jnp.where(rim_codes == code_value, rim_weights, jnp.zeros_like(rim_weights)), axis=0
            )
            entries.append((row_shift, col_shift, weight))
    return (entries, jnp.sum(rim_weights, axis=0))


def charges(spike_bins, efficacy, is_live, step_values):
    trials, regions, slot_count = spike_bins.shape
    bins_moved = jnp.transpose(spike_bins, (1, 2, 0))
    elapsed = (step_values[None, None, :, None] - bins_moved[:, :, None, :]).astype(jnp.float32)
    has_fired = (bins_moved[:, :, None, :] <= step_values[None, None, :, None]) & is_live[
        :, :, None, None
    ]
    values = jnp.where(
        has_fired,
        efficacy.astype(jnp.float32)[:, :, None, None] * jnp.exp(-0.35 * elapsed),
        jnp.zeros_like(elapsed),
    )
    return values.astype(jnp.bfloat16).reshape(regions * slot_count, step_values.shape[0] * trials)


def band_matrix(sites_region, row_count, total_sites):
    kernel = footprint()
    columns = jnp.arange(row_count, dtype=jnp.int32)
    distance = (columns[None, :] - sites_region[:, None]) % total_sites
    matrix = jnp.zeros(distance.shape, jnp.float32)
    for offset in range(FOOT):
        matrix = matrix + jnp.where(distance == offset, kernel[offset], jnp.float32(0.0))
    return matrix


def band_spreader(charge_rows, site_ids, total_sites, row_width, row_count):
    regions, slot_count = site_ids.shape
    values = (
        lax.optimization_barrier(charge_rows)
        .astype(jnp.float32)
        .reshape(regions, slot_count, row_width)
    )

    def one_region(inputs):
        sites_region, values_region = inputs
        matrix = band_matrix(sites_region, row_count, total_sites)
        return jnp.einsum(
            "jv,jw->vw",
            matrix,
            values_region,
            precision=lax.Precision.HIGHEST,
            preferred_element_type=jnp.float32,
        )

    by_region = lax.map(one_region, (site_ids, values))
    return jnp.transpose(by_region, (1, 0, 2)).reshape(row_count, regions * row_width)


def band_collector(site_ids, total_sites, row_width, block_rows):
    regions = site_ids.shape[0]
    length = block_rows.shape[0]
    by_region = jnp.transpose(block_rows.reshape(length, regions, row_width), (1, 0, 2)).astype(
        jnp.float32
    )

    def one_region(inputs):
        sites_region, rows_region = inputs
        matrix = band_matrix(sites_region, length, total_sites)
        return jnp.dot(
            matrix, rows_region, precision=lax.Precision.HIGHEST, preferred_element_type=jnp.float32
        )

    return lax.map(one_region, (site_ids, by_region))


def apply_stencil(field_now, full_field, rate_now, entries, weight_sum):
    regions = field_now.shape[1]
    sites_here = field_now.shape[2]
    spread_sum = -weight_sum * field_now
    for row_shift, col_shift, weight in entries:
        spread_sum = (
            spread_sum
            + weight
            * full_field[
                :,
                RIM + row_shift : RIM + row_shift + regions,
                RIM + col_shift : RIM + col_shift + sites_here,
            ]
        )
    return 0.9 * field_now + 0.15 * spread_sum + 0.1 * rate_now


def advance(field_now, rate_now, entries, weight_sum):
    wide_field = padded(field_now, (("surf", 2),), RIM, True)
    full_field = padded(wide_field, (("neur", 1),), RIM, False)
    return apply_stencil(field_now, full_field, rate_now, entries, weight_sum)


def local(
    spike_bins,
    neuron_site,
    efficacy,
    region_live,
    membrane_init,
    field_init,
    rim_weights,
    rim_codes,
):
    trials, regions, slot_count = spike_bins.shape
    sites_here = field_init.shape[2]
    total_sites = sites_here * lax.axis_size("surf")
    slot_ids = lax.axis_index("surf") * slot_count + jnp.arange(slot_count, dtype=jnp.int32)
    is_live = slot_ids[None, :] < region_live[:, None]
    entries, weight_sum = stencil(rim_weights, rim_codes)
    step_values = jnp.arange(STEPS, dtype=jnp.int32)
    charge_rows = charges(spike_bins, efficacy, is_live, step_values)
    row_width = STEPS * trials
    rate_rows = lax.psum_scatter(
        band_spreader(
            charge_rows, neuron_site, total_sites, row_width, sites_here * lax.axis_size("surf")
        ).astype(jnp.bfloat16),
        "surf",
        scatter_dimension=0,
        tiled=True,
    ).astype(jnp.float32)
    rate_steps = jnp.transpose(rate_rows.reshape(sites_here, regions, STEPS, trials), (2, 3, 1, 0))

    def field_step(field_now, rate_now):
        field_next = advance(field_now, rate_now, entries, weight_sum)
        return (field_next, field_next.astype(jnp.bfloat16))

    field_final, history = lax.scan(field_step, field_init, rate_steps)
    history_rows = jnp.transpose(history, (3, 2, 0, 1)).reshape(sites_here, regions * row_width)
    neuron_drive = band_collector(
        neuron_site,
        total_sites,
        row_width,
        lax.all_gather(history_rows, "surf", axis=0, tiled=True),
    )
    neuron_drive = jnp.transpose(
        neuron_drive.reshape(regions, slot_count, STEPS, trials), (2, 3, 0, 1)
    )

    def membrane_step(voltage, inputs):
        drive_now, step_index = inputs
        voltage = 0.9 * voltage + 0.5 * drive_now
        return (jnp.where(spike_bins == step_index, -0.5 * jnp.ones_like(voltage), voltage), None)

    voltage, unused = lax.scan(membrane_step, membrane_init, (neuron_drive, step_values))
    membranes = jnp.where(is_live[None, :, :], voltage, jnp.zeros_like(voltage))
    return (field_final, membranes)


def solution(mesh):
    in_specs = (
        P(None, "neur", "surf"),
        P("neur", "surf"),
        P("neur", "surf"),
        P("neur"),
        P(None, "neur", "surf"),
        P(None, "neur", "surf"),
        P(None, "neur", "surf"),
        P(None, "neur", "surf"),
    )
    out_specs = (P(None, "neur", "surf"), P(None, "neur", "surf"))
    return jax.shard_map(local, mesh=mesh, in_specs=in_specs, out_specs=out_specs, check_vma=False)
```

profile of v0, /device:TPU:1, one launch (start us, length us, event | category | flops | bytes accessed | tf_op | source)
XLA Modules:
  0.0 849.3 jit_solution(10700092418684364237)
XLA Ops:
  9.7 6.6 copy.56
  16.5 4.5 select_convert_fusion
  21.0 4.9 copy.24
  25.9 141.1 %while.48 = (s32[]{:T(128)}, bf16[8,1024,160]{1,2,0:T(8,128)(2,1)}, s32[8,1024]{1,0:T(8,128)}, f32[8,1024,160]{2,1,0:T(8,128)}, s32[]{:T(128)}) while((s32[]{:T(128)}, bf16[8,1024,160]{1,2,0:T(8,128)(2,1)}, s32[8,1024]{1,0:T(8,128)}, f32[8,1024,160]{2,1,0:T(8,128)}, s32[]{:T(128)}) %tuple.162), condition=%wide.region_2.3_spmd, body=%wide.region_0.0_spmd.sunk | while | flops 2049966080 | bytes 1721513 | solution.py:88
  28.6 14.9 %fusion.189 = bf16[8,1024,160]{1,2,0:T(8,128)(2,1)} fusion(bf16[8,1024,160]{1,2,0:T(8,128)(2,1)} %get-tuple-element.985, s32[]{:T(128)} %get-tuple-element.984, f32[]{:T(128)} %bitcast.108, f32[]{:T(128)} %bitcast.109, f32[]{:T(128)} %bitcast.110, f32[]{:T(128)} %bitcast.111, f32[]{:T(128)} %bitcast.112, f32[]{:T(128)} %bitcast.113, f32[]{:T(128)} %bitcast.114, ...), kind=kOutput, calls=%fused_computation.52.clone.1 | convolution fusion | flops 2049966080 | bytes 1713152 | tf_op jit(solution)/shard_map/while/body/eval_jaxpr/jv,jw->vw/dot_general | solution.py:80
  46.3 14.9 %fusion.189 = bf16[8,1024,160]{1,2,0:T(8,128)(2,1)} fusion(bf16[8,1024,160]{1,2,0:T(8,128)(2,1)} %get-tuple-element.985, s32[]{:T(128)} %get-tuple-element.984, f32[]{:T(128)} %bitcast.108, f32[]{:T(128)} %bitcast.109, f32[]{:T(128)} %bitcast.110, f32[]{:T(128)} %bitcast.111, f32[]{:T(128)} %bitcast.112, f32[]{:T(128)} %bitcast.113, f32[]{:T(128)} %bitcast.114, ...), kind=kOutput, calls=%fused_computation.52.clone.1 | convolution fusion | flops 2049966080 | bytes 1713152 | tf_op jit(solution)/shard_map/while/body/eval_jaxpr/jv,jw->vw/dot_general | solution.py:80
  63.9 14.9 %fusion.189 = bf16[8,1024,160]{1,2,0:T(8,128)(2,1)} fusion(bf16[8,1024,160]{1,2,0:T(8,128)(2,1)} %get-tuple-element.985, s32[]{:T(128)} %get-tuple-element.984, f32[]{:T(128)} %bitcast.108, f32[]{:T(128)} %bitcast.109, f32[]{:T(128)} %bitcast.110, f32[]{:T(128)} %bitcast.111, f32[]{:T(128)} %bitcast.112, f32[]{:T(128)} %bitcast.113, f32[]{:T(128)} %bitcast.114, ...), kind=kOutput, calls=%fused_computation.52.clone.1 | convolution fusion | flops 2049966080 | bytes 1713152 | tf_op jit(solution)/shard_map/while/body/eval_jaxpr/jv,jw->vw/dot_general | solution.py:80
  81.6 14.9 %fusion.189 = bf16[8,1024,160]{1,2,0:T(8,128)(2,1)} fusion(bf16[8,1024,160]{1,2,0:T(8,128)(2,1)} %get-tuple-element.985, s32[]{:T(128)} %get-tuple-element.984, f32[]{:T(128)} %bitcast.108, f32[]{:T(128)} %bitcast.109, f32[]{:T(128)} %bitcast.110, f32[]{:T(128)} %bitcast.111, f32[]{:T(128)} %bitcast.112, f32[]{:T(128)} %bitcast.113, f32[]{:T(128)} %bitcast.114, ...), kind=kOutput, calls=%fused_computation.52.clone.1 | convolution fusion | flops 2049966080 | bytes 1713152 | tf_op jit(solution)/shard_map/while/body/eval_jaxpr/jv,jw->vw/dot_general | solution.py:80
  99.2 14.9 %fusion.189 = bf16[8,1024,160]{1,2,0:T(8,128)(2,1)} fusion(bf16[8,1024,160]{1,2,0:T(8,128)(2,1)} %get-tuple-element.985, s32[]{:T(128)} %get-tuple-element.984, f32[]{:T(128)} %bitcast.108, f32[]{:T(128)} %bitcast.109, f32[]{:T(128)} %bitcast.110, f32[]{:T(128)} %bitcast.111, f32[]{:T(128)} %bitcast.112, f32[]{:T(128)} %bitcast.113, f32[]{:T(128)} %bitcast.114, ...), kind=kOutput, calls=%fused_computation.52.clone.1 | convolution fusion | flops 2049966080 | bytes 1713152 | tf_op jit(solution)/shard_map/while/body/eval_jaxpr/jv,jw->vw/dot_general | solution.py:80
  116.8 14.9 %fusion.189 = bf16[8,1024,160]{1,2,0:T(8,128)(2,1)} fusion(bf16[8,1024,160]{1,2,0:T(8,128)(2,1)} %get-tuple-element.985, s32[]{:T(128)} %get-tuple-element.984, f32[]{:T(128)} %bitcast.108, f32[]{:T(128)} %bitcast.109, f32[]{:T(128)} %bitcast.110, f32[]{:T(128)} %bitcast.111, f32[]{:T(128)} %bitcast.112, f32[]{:T(128)} %bitcast.113, f32[]{:T(128)} %bitcast.114, ...), kind=kOutput, calls=%fused_computation.52.clone.1 | convolution fusion | flops 2049966080 | bytes 1713152 | tf_op jit(solution)/shard_map/while/body/eval_jaxpr/jv,jw->vw/dot_general | solution.py:80
  134.4 14.9 %fusion.189 = bf16[8,1024,160]{1,2,0:T(8,128)(2,1)} fusion(bf16[8,1024,160]{1,2,0:T(8,128)(2,1)} %get-tuple-element.985, s32[]{:T(128)} %get-tuple-element.984, f32[]{:T(128)} %bitcast.108, f32[]{:T(128)} %bitcast.109, f32[]{:T(128)} %bitcast.110, f32[]{:T(128)} %bitcast.111, f32[]{:T(128)} %bitcast.112, f32[]{:T(128)} %bitcast.113, f32[]{:T(128)} %bitcast.114, ...), kind=kOutput, calls=%fused_computation.52.clone.1 | convolution fusion | flops 2049966080 | bytes 1713152 | tf_op jit(solution)/shard_map/while/body/eval_jaxpr/jv,jw->vw/dot_general | solution.py:80
  152.1 14.9 %fusion.189 = bf16[8,1024,160]{1,2,0:T(8,128)(2,1)} fusion(bf16[8,1024,160]{1,2,0:T(8,128)(2,1)} %get-tuple-element.985, s32[]{:T(128)} %get-tuple-element.984, f32[]{:T(128)} %bitcast.108, f32[]{:T(128)} %bitcast.109, f32[]{:T(128)} %bitcast.110, f32[]{:T(128)} %bitcast.111, f32[]{:T(128)} %bitcast.112, f32[]{:T(128)} %bitcast.113, f32[]{:T(128)} %bitcast.114, ...), kind=kOutput, calls=%fused_computation.52.clone.1 | convolution fusion | flops 2049966080 | bytes 1713152 | tf_op jit(solution)/shard_map/while/body/eval_jaxpr/jv,jw->vw/dot_general | solution.py:80
  167.0 4.4 copy.25
  171.6 119.9 %reduce-scatter.4.cloned.1.call-done = bf16[32,1280]{1,0:T(8,128)(2,1)} async-done(((bf16[1024,1280]{1,0:T(8,128)(2,1)}), bf16[32,1280]{1,0:T(8,128)(2,1)}) %reduce-scatter.4.cloned.1.call-update) | async-done | bytes 81936
  292.7 173.5 %while.49 = (s32[]{:T(128)}, f32[16,8,32]{2,1,0:T(8,128)S(1)}, bf16[10,16,8,32]{3,2,1,0:T(8,128)(2,1)S(1)}, f32[1,8,32]{2,1,0:T(8,128)S(1)}, f32[8,32]{1,0:T(8,1...) while((s32[]{:T(128)}, f32[16,8,32]{2,1,0:T(8,128)S(1)}, ...), condition=%wide.region_30.31_spmd, body=%wide.region_29.30_spmd.sunk | while | flops 280834 | bytes 1990069 | solution.py:165
  292.8 5.8 collective-permute-start
  305.7 3.7 collective-permute-done.3
  310.2 5.3 collective-permute-start
  317.2 4.4 collective-permute-start.2
  326.9 7.5 collective-permute-start
  344.1 7.3 collective-permute-start
  352.9 4.5 collective-permute-start.2
  362.7 7.5 collective-permute-start
  379.7 7.6 collective-permute-start
  388.8 3.9 collective-permute-start.2
  398.1 7.5 collective-permute-start
  415.7 7.5 collective-permute-start
  432.6 7.5 collective-permute-start
  449.5 7.5 collective-permute-start
  467.2 84.4 %all-gather.2.cloned.1.call-done = bf16[1024,1280]{1,0:T(8,128)(2,1)} async-done(((bf16[32,1280]{1,0:T(8,128)(2,1)}), bf16[1024,1280]{1,0:T(8,128)(2,1)}) %all-gather.2.cloned.1.call-update) | async-done | bytes 2621456 | tf_op jit(solution)/shard_map/all_gather | solution.py:171
  557.6 257.9 %while.50 = (s32[]{:T(128)}, f32[8,1024,160]{1,0,2:T(8,128)}, s32[8,1024]{1,0:T(8,128)}, f32[8,1024,160]{1,2,0:T(8,128)}, s32[]{:T(128)}, /*index=5*/s32[]{:T(128)}) while((s32[]{:T(128)}, f32[8,1024,160]{1,0,2:T(8,128)}, s32[8,1024]{1,0:T(8,128)}, f32[8,1024,160]{1,2,0:T(8,128)}, s32[]{:T(128)}, /*index=5*/s32[]{:T(128)}) %tuple.165), condition=%wide.region_33.34_spmd, body=%wide.region_31.33_spmd.sunk | while | flops 2049966080 | bytes 3949237 | solution.py:106
  560.3 15.5 %fusion.196 = f32[1,1024,160]{1,2,0:T(8,128)S(1)} fusion(f32[]{:T(128)} %bitcast.121, f32[]{:T(128)} %bitcast.122, f32[]{:T(128)} %bitcast.123, f32[]{:T(128)} %bitcast.124, f32[]{:T(128)} %bitcast.125, f32[]{:T(128)} %bitcast.126, f32[]{:T(128)} %bitcast.127, f32[]{:T(128)} %bitcast.128, s32[1024]{0:T(1024)S(1)} %bitcast.146, ...), kind=kOutput, calls=%fused_computation.183.clone.1 | convolution fusion | flops 2049966080 | bytes 1319424 | tf_op jit(solution)/shard_map/while/body/eval_jaxpr/dot_general | solution.py:102
  576.5 13.4 %dynamic_update_slice.26 = f32[8,1024,160]{1,0,2:T(8,128)} dynamic-update-slice(f32[8,1024,160]{1,0,2:T(8,128)} %get-tuple-element.1091, f32[1,1024,160]{1,0,2:T(1,128)S(1)} %copy.69, s32[]{:T(128)} %get-tuple-element.1090, s32[]{:T(128)} %constant.232.clone.1..sunk, s32[]{:T(128)} %constant.232.clone.1..sunk) | dynamic-update-slice | bytes 1310724 | tf_op jit(solution)/shard_map/while/body/jit(dynamic_update_index_in_dim)/dynamic_update_slice | solution.py:88
  592.5 15.5 %fusion.196 = f32[1,1024,160]{1,2,0:T(8,128)S(1)} fusion(f32[]{:T(128)} %bitcast.121, f32[]{:T(128)} %bitcast.122, f32[]{:T(128)} %bitcast.123, f32[]{:T(128)} %bitcast.124, f32[]{:T(128)} %bitcast.125, f32[]{:T(128)} %bitcast.126, f32[]{:T(128)} %bitcast.127, f32[]{:T(128)} %bitcast.128, s32[1024]{0:T(1024)S(1)} %bitcast.146, ...), kind=kOutput, calls=%fused_computation.183.clone.1 | convolution fusion | flops 2049966080 | bytes 1319424 | tf_op jit(solution)/shard_map/while/body/eval_jaxpr/dot_general | solution.py:102
  608.7 13.4 %dynamic_update_slice.26 = f32[8,1024,160]{1,0,2:T(8,128)} dynamic-update-slice(f32[8,1024,160]{1,0,2:T(8,128)} %get-tuple-element.1091, f32[1,1024,160]{1,0,2:T(1,128)S(1)} %copy.69, s32[]{:T(128)} %get-tuple-element.1090, s32[]{:T(128)} %constant.232.clone.1..sunk, s32[]{:T(128)} %constant.232.clone.1..sunk) | dynamic-update-slice | bytes 1310724 | tf_op jit(solution)/shard_map/while/body/jit(dynamic_update_index_in_dim)/dynamic_update_slice | solution.py:88
  624.8 15.5 %fusion.196 = f32[1,1024,160]{1,2,0:T(8,128)S(1)} fusion(f32[]{:T(128)} %bitcast.121, f32[]{:T(128)} %bitcast.122, f32[]{:T(128)} %bitcast.123, f32[]{:T(128)} %bitcast.124, f32[]{:T(128)} %bitcast.125, f32[]{:T(128)} %bitcast.126, f32[]{:T(128)} %bitcast.127, f32[]{:T(128)} %bitcast.128, s32[1024]{0:T(1024)S(1)} %bitcast.146, ...), kind=kOutput, calls=%fused_computation.183.clone.1 | convolution fusion | flops 2049966080 | bytes 1319424 | tf_op jit(solution)/shard_map/while/body/eval_jaxpr/dot_general | solution.py:102
  640.9 13.4 %dynamic_update_slice.26 = f32[8,1024,160]{1,0,2:T(8,128)} dynamic-update-slice(f32[8,1024,160]{1,0,2:T(8,128)} %get-tuple-element.1091, f32[1,1024,160]{1,0,2:T(1,128)S(1)} %copy.69, s32[]{:T(128)} %get-tuple-element.1090, s32[]{:T(128)} %constant.232.clone.1..sunk, s32[]{:T(128)} %constant.232.clone.1..sunk) | dynamic-update-slice | bytes 1310724 | tf_op jit(solution)/shard_map/while/body/jit(dynamic_update_index_in_dim)/dynamic_update_slice | solution.py:88
  657.0 15.5 %fusion.196 = f32[1,1024,160]{1,2,0:T(8,128)S(1)} fusion(f32[]{:T(128)} %bitcast.121, f32[]{:T(128)} %bitcast.122, f32[]{:T(128)} %bitcast.123, f32[]{:T(128)} %bitcast.124, f32[]{:T(128)} %bitcast.125, f32[]{:T(128)} %bitcast.126, f32[]{:T(128)} %bitcast.127, f32[]{:T(128)} %bitcast.128, s32[1024]{0:T(1024)S(1)} %bitcast.146, ...), kind=kOutput, calls=%fused_computation.183.clone.1 | convolution fusion | flops 2049966080 | bytes 1319424 | tf_op jit(solution)/shard_map/while/body/eval_jaxpr/dot_general | solution.py:102
  673.2 13.4 %dynamic_update_slice.26 = f32[8,1024,160]{1,0,2:T(8,128)} dynamic-update-slice(f32[8,1024,160]{1,0,2:T(8,128)} %get-tuple-element.1091, f32[1,1024,160]{1,0,2:T(1,128)S(1)} %copy.69, s32[]{:T(128)} %get-tuple-element.1090, s32[]{:T(128)} %constant.232.clone.1..sunk, s32[]{:T(128)} %constant.232.clone.1..sunk) | dynamic-update-slice | bytes 1310724 | tf_op jit(solution)/shard_map/while/body/jit(dynamic_update_index_in_dim)/dynamic_update_slice | solution.py:88
  689.2 15.5 %fusion.196 = f32[1,1024,160]{1,2,0:T(8,128)S(1)} fusion(f32[]{:T(128)} %bitcast.121, f32[]{:T(128)} %bitcast.122, f32[]{:T(128)} %bitcast.123, f32[]{:T(128)} %bitcast.124, f32[]{:T(128)} %bitcast.125, f32[]{:T(128)} %bitcast.126, f32[]{:T(128)} %bitcast.127, f32[]{:T(128)} %bitcast.128, s32[1024]{0:T(1024)S(1)} %bitcast.146, ...), kind=kOutput, calls=%fused_computation.183.clone.1 | convolution fusion | flops 2049966080 | bytes 1319424 | tf_op jit(solution)/shard_map/while/body/eval_jaxpr/dot_general | solution.py:102
  705.4 13.4 %dynamic_update_slice.26 = f32[8,1024,160]{1,0,2:T(8,128)} dynamic-update-slice(f32[8,1024,160]{1,0,2:T(8,128)} %get-tuple-element.1091, f32[1,1024,160]{1,0,2:T(1,128)S(1)} %copy.69, s32[]{:T(128)} %get-tuple-element.1090, s32[]{:T(128)} %constant.232.clone.1..sunk, s32[]{:T(128)} %constant.232.clone.1..sunk) | dynamic-update-slice | bytes 1310724 | tf_op jit(solution)/shard_map/while/body/jit(dynamic_update_index_in_dim)/dynamic_update_slice | solution.py:88
  721.5 15.5 %fusion.196 = f32[1,1024,160]{1,2,0:T(8,128)S(1)} fusion(f32[]{:T(128)} %bitcast.121, f32[]{:T(128)} %bitcast.122, f32[]{:T(128)} %bitcast.123, f32[]{:T(128)} %bitcast.124, f32[]{:T(128)} %bitcast.125, f32[]{:T(128)} %bitcast.126, f32[]{:T(128)} %bitcast.127, f32[]{:T(128)} %bitcast.128, s32[1024]{0:T(1024)S(1)} %bitcast.146, ...), kind=kOutput, calls=%fused_computation.183.clone.1 | convolution fusion | flops 2049966080 | bytes 1319424 | tf_op jit(solution)/shard_map/while/body/eval_jaxpr/dot_general | solution.py:102
  737.6 13.4 %dynamic_update_slice.26 = f32[8,1024,160]{1,0,2:T(8,128)} dynamic-update-slice(f32[8,1024,160]{1,0,2:T(8,128)} %get-tuple-element.1091, f32[1,1024,160]{1,0,2:T(1,128)S(1)} %copy.69, s32[]{:T(128)} %get-tuple-element.1090, s32[]{:T(128)} %constant.232.clone.1..sunk, s32[]{:T(128)} %constant.232.clone.1..sunk) | dynamic-update-slice | bytes 1310724 | tf_op jit(solution)/shard_map/while/body/jit(dynamic_update_index_in_dim)/dynamic_update_slice | solution.py:88
  753.7 15.5 %fusion.196 = f32[1,1024,160]{1,2,0:T(8,128)S(1)} fusion(f32[]{:T(128)} %bitcast.121, f32[]{:T(128)} %bitcast.122, f32[]{:T(128)} %bitcast.123, f32[]{:T(128)} %bitcast.124, f32[]{:T(128)} %bitcast.125, f32[]{:T(128)} %bitcast.126, f32[]{:T(128)} %bitcast.127, f32[]{:T(128)} %bitcast.128, s32[1024]{0:T(1024)S(1)} %bitcast.146, ...), kind=kOutput, calls=%fused_computation.183.clone.1 | convolution fusion | flops 2049966080 | bytes 1319424 | tf_op jit(solution)/shard_map/while/body/eval_jaxpr/dot_general | solution.py:102
  769.9 13.4 %dynamic_update_slice.26 = f32[8,1024,160]{1,0,2:T(8,128)} dynamic-update-slice(f32[8,1024,160]{1,0,2:T(8,128)} %get-tuple-element.1091, f32[1,1024,160]{1,0,2:T(1,128)S(1)} %copy.69, s32[]{:T(128)} %get-tuple-element.1090, s32[]{:T(128)} %constant.232.clone.1..sunk, s32[]{:T(128)} %constant.232.clone.1..sunk) | dynamic-update-slice | bytes 1310724 | tf_op jit(solution)/shard_map/while/body/jit(dynamic_update_index_in_dim)/dynamic_update_slice | solution.py:88
  785.9 15.5 %fusion.196 = f32[1,1024,160]{1,2,0:T(8,128)S(1)} fusion(f32[]{:T(128)} %bitcast.121, f32[]{:T(128)} %bitcast.122, f32[]{:T(128)} %bitcast.123, f32[]{:T(128)} %bitcast.124, f32[]{:T(128)} %bitcast.125, f32[]{:T(128)} %bitcast.126, f32[]{:T(128)} %bitcast.127, f32[]{:T(128)} %bitcast.128, s32[1024]{0:T(1024)S(1)} %bitcast.146, ...), kind=kOutput, calls=%fused_computation.183.clone.1 | convolution fusion | flops 2049966080 | bytes 1319424 | tf_op jit(solution)/shard_map/while/body/eval_jaxpr/dot_general | solution.py:102
  802.1 13.4 %dynamic_update_slice.26 = f32[8,1024,160]{1,0,2:T(8,128)} dynamic-update-slice(f32[8,1024,160]{1,0,2:T(8,128)} %get-tuple-element.1091, f32[1,1024,160]{1,0,2:T(1,128)S(1)} %copy.69, s32[]{:T(128)} %get-tuple-element.1090, s32[]{:T(128)} %constant.232.clone.1..sunk, s32[]{:T(128)} %constant.232.clone.1..sunk) | dynamic-update-slice | bytes 1310724 | tf_op jit(solution)/shard_map/while/body/jit(dynamic_update_index_in_dim)/dynamic_update_slice | solution.py:88
  815.5 26.1 %while.51 = (s32[]{:T(128)}, f32[16,8,1024]{2,1,0:T(8,128)S(1)}, s32[10]{0:T(128)S(1)}, s32[16,8,1024]{2,1,0:T(8,128)S(1)}, f32[10,16,8,1024]{3,2,1,0:T(8,128)}, /*index=5*/s32[]{:T(128)}) while((s32[]{:T(128)}, f32[16,8,1024]{2,1,0:T(8,128)S(1)}, s32[10]{0:T(128)S(1)}, s32[16,8,1024]{2,1,0:T(8,128)S(1)}, f32[10,16,8,1024]{3,2,1,0:T(8,128)}, ...), condition=%wide.region_35.36_spmd, body=%wide.region_34.35_spmd.sunk | while | flops 655362 | bytes 2097241 | solution.py:182
  (261 shorter events, 171.2 us)
Async XLA Ops:
  7.2 284.3 %reduce-scatter.4.cloned.1.call-start = ((), (), s32[]{:S(2)}) async-start(), calls=%async_computation.2 | async-start | bytes 2703360
  9.7 6.7 copy-start.6
  167.0 125.7 %copy-start.3 = (f32[16,8,32]{2,1,0:T(8,128)S(1)}, f32[16,8,32]{2,1,0:T(8,128)}, u32[]{:S(2)}) copy-start(f32[16,8,32]{2,1,0:T(8,128)} %param.21) | copy-start | bytes 49156
  171.4 380.2 %all-gather.2.cloned.1.call-start = ((), (), s32[]{:S(2)}) async-start(), calls=%async_computation.1 | async-start | bytes 2703360 | tf_op jit(solution)/shard_map/all_gather | solution.py:171
  292.7 174.4 %copy-start.7 = (s32[8]{0:T(128)S(1)}, s32[8]{0:T(128)}, u32[]{:S(2)}) copy-start(s32[8]{0:T(128)} %param.19) | copy-start | bytes 100
  292.8 9.1 %collective-permute-start = (f32[16,8,2]{2,1,0:T(8,128)S(1)}, f32[16,8,2]{2,1,0:T(8,128)S(1)}, u32[]{:S(2)}, u32[]{:S(2)}) collective-permute-start(f32[16,8,2]{2,1,0:T(8,128)S(1)} %get-tuple-element.954), channel_id=1, source_target_pairs={{8,0},{16,8},{24,16},{32,24},{40,32},{48,40},{56,48},{64,56},{72,6... | collective-permute-start | bytes 3080 | tf_op jit(solution)/shard_map/while/body/eval_jaxpr/ppermute | solution.py:19
  298.7 3.3 collective-permute-start.1
  302.1 3.6 collective-permute-start.2
  304.4 5.0 collective-permute-start.3
  310.2 6.8 collective-permute-start
  315.5 1.5 collective-permute-start.1
  317.2 5.7 collective-permute-start.2
  321.6 4.5 collective-permute-start.3
  326.9 8.4 collective-permute-start
  334.4 1.3 collective-permute-start.1
  335.9 3.9 collective-permute-start.2
  338.5 4.8 collective-permute-start.3
  344.1 8.2 collective-permute-start
  351.4 1.3 collective-permute-start.1
  352.9 5.9 collective-permute-start.2
  357.4 4.5 collective-permute-start.3
  362.7 8.4 collective-permute-start
  370.2 1.3 collective-permute-start.1
  371.7 4.0 collective-permute-start.2
  374.4 4.5 collective-permute-start.3
  379.7 8.5 %collective-permute-start = (f32[16,8,2]{2,1,0:T(8,128)S(1)}, f32[16,8,2]{2,1,0:T(8,128)S(1)}, u32[]{:S(2)}, u32[]{:S(2)}) collective-permute-start(f32[16,8,2]{2,1,0:T(8,128)S(1)} %get-tuple-element.954), channel_id=1, source_target_pairs={{8,0},{16,8},{24,16},{32,24},{40,32},{48,40},{56,48},{64,56},{72,6... | collective-permute-start | bytes 3080 | tf_op jit(solution)/shard_map/while/body/eval_jaxpr/ppermute | solution.py:19
  387.3 1.3 collective-permute-start.1
  388.8 5.3 collective-permute-start.2
  392.8 4.5 collective-permute-start.3
  398.1 8.4 collective-permute-start
  405.6 1.3 collective-permute-start.1
  407.1 4.6 collective-permute-start.2
  410.4 4.5 collective-permute-start.3
  415.7 8.4 collective-permute-start
  423.3 1.3 collective-permute-start.1
  424.7 3.9 collective-permute-start.2
  427.3 4.5 collective-permute-start.3
  432.6 8.4 collective-permute-start
  440.1 1.3 collective-permute-start.1
  441.6 3.9 collective-permute-start.2
  444.2 4.5 collective-permute-start.3
  449.5 8.4 collective-permute-start
  457.0 1.3 collective-permute-start.1
  458.5 3.9 collective-permute-start.2
  461.0 4.5 collective-permute-start.3
  466.2 91.4 %copy-start.2 = (f32[16,8,32]{2,1,0:T(8,128)}, f32[16,8,32]{2,1,0:T(8,128)S(1)}, u32[]{:S(2)}) copy-start(f32[16,8,32]{2,1,0:T(8,128)S(1)} %get-tuple-element.461) | copy-start | bytes 49156
  557.6 257.9 %copy-start = (f32[16,8,1024]{2,1,0:T(8,128)S(1)}, f32[16,8,1024]{2,1,0:T(8,128)}, u32[]{:S(2)}) copy-start(f32[16,8,1024]{2,1,0:T(8,128)} %param.20) | copy-start | bytes 1572868
  557.6 257.9 %copy-start.1 = (s32[16,8,1024]{2,1,0:T(8,128)S(1)}, s32[16,8,1024]{2,1,0:T(8,128)}, u32[]{:S(2)}) copy-start(s32[16,8,1024]{2,1,0:T(8,128)} %param.16) | copy-start | bytes 1572868
  (2 other events, 9.0 us)
Sparse Core Ops, SparseCore 0:
  171.6 119.9 reduce-scatter.3
  467.2 84.3 all-gather.1
where the time goes:
time: 856 us; the launch traced here: 849 us
  waiting for transfers between devices  251 us (29%)
  matrix products  243 us (28%)
  local copies, waits for them, and re-layouts  166 us (19%)
  starting transfers between devices  117 us (14%)
  other arithmetic  57.4 us (7%)
  between operations  14.2 us (2%)
    dot_general x8, matrix products, one_region(): jnp.dot(matrix, rows_region, precision=lax.Precision.HIGHEST, preferred_e...  124 us
    unnamed x3, waiting for transfers between devices  120 us
    dot_general x8, matrix products, one_region(): jnp.einsum('jv,jw->vw', matrix, values_region, precision=lax.Precision.HI...  119 us
    dynamic_update_slice x16, local copies, waits for them, and re-layouts, band_spreader(): by_region = lax.map(one_region, (site_ids, values))  112 us
    all_gather x1, waiting for transfers between devices, local(): lax.all_gather(history_rows, 'surf', axis=0, tiled=True)  84.4 us
    ppermute x20, starting transfers between devices, padded(): after = lax.ppermute(leading, axis, down)  84.2 us
    ppermute x20, waiting for transfers between devices, padded(): after = lax.ppermute(leading, axis, down)  42.9 us
    ppermute x20, starting transfers between devices, padded(): before = lax.ppermute(last, axis, up)  32.8 us
  transfers between devices with their start and end apart: 42, of which 30 were waited for; matrix products, arithmetic and copies ran while one was open for 0% of the time, Pallas kernels for 0%

commit v1 on v0

v1 whole, which is shorter than its diff:
```python
import math

import jax
import jax.numpy as jnp
from jax import lax
from jax.experimental import pallas as pl
from jax.experimental.pallas import tpu as pltpu
from jax.sharding import PartitionSpec as P

STEPS = 10
RIM = 2
FOOT = 8
TAPS = (0.84375, 0.51171875, 0.310546875, 0.1884765625, 0.1142578125, 0.0693359375, 0.0419921875, 0.025390625)
SCALE = 1.0 / sum(TAPS)
DECAY = math.exp(-0.35)
F32 = jnp.float32
BF16 = jnp.bfloat16
VMEM_LIMIT = 56 * 1024 * 1024
ROWS = 80
LANES = 128


def build_band(site, band_ref):
    total, slots = band_ref.shape
    tiles = total // 16
    high = jnp.broadcast_to((site >> 4).astype(F32).astype(BF16), (16, slots))
    low = jnp.broadcast_to(site & 15, (16, slots))
    row = lax.broadcasted_iota(jnp.int32, (16, slots), 0)
    first = jnp.zeros((16, slots), F32)
    second = jnp.zeros((16, slots), F32)
    for offset in range(FOOT):
        first = jnp.where(row - low == offset, TAPS[offset], first)
        second = jnp.where(row + 16 - low == offset, TAPS[offset], second)
    first, second = first.astype(BF16), second.astype(BF16)
    zero = jnp.zeros((16, slots), BF16)
    for tile in range(tiles):
        here = high == jnp.asarray(tile, BF16)
        before = high == jnp.asarray((tile - 1) % tiles, BF16)
        band_ref[tile * 16 : tile * 16 + 16, :] = jnp.where(here, first, jnp.where(before, second, zero))


def spread_kernel(live_ref, bins_ref, site_ref, eff_ref, out_ref, band_ref):
    region = pl.program_id(0)
    slots = site_ref.shape[1]
    slot = lax.axis_index("surf") * slots + lax.broadcasted_iota(jnp.int32, (1, slots), 1)
    weight = jnp.where(slot < live_ref[region], eff_ref[pl.ds(region, 1), :], 0.0)
    weight = jnp.broadcast_to(weight, (8, slots))
    build_band(site_ref[pl.ds(region, 1), :], band_ref)
    rows = []
    for half in range(2):
        bins = bins_ref[half, :, 0, 0]
        for step in range(STEPS):
            rows.append(jnp.where(bins == step, weight, 0.0))
    charge = jnp.concatenate(rows, axis=0).astype(BF16)
    total = lax.dot_general(charge, band_ref[...], (((1,), (1,)), ((), ())), preferred_element_type=F32)
    total = (total * SCALE).astype(BF16)
    for plane in range(8):
        for half in range(2):
            out_ref[plane, half, 0] = total[half * ROWS : half * ROWS + ROWS, plane * LANES : plane * LANES + LANES]


def collect_kernel(live_ref, gather_ref, bins_ref, site_ref, init_ref, out_ref, band_ref):
    region = pl.program_id(0)
    slots = site_ref.shape[1]
    slot = lax.axis_index("surf") * slots + lax.broadcasted_iota(jnp.int32, (8, slots), 1)
    live = slot < live_ref[region]
    build_band(site_ref[pl.ds(region, 1), :], band_ref)
    history = jnp.concatenate(
        [jnp.concatenate([gather_ref[plane, 0, 0], gather_ref[plane, 1, 0]], axis=0) for plane in range(8)], axis=1
    )
    drive = jnp.dot(history, band_ref[...], preferred_element_type=F32)
    for half in range(2):
        bins = bins_ref[half, :, 0, 0]
        voltage = init_ref[half, :, 0, 0]
        for step in range(STEPS):
            start = half * ROWS + step * 8
            voltage = 0.9 * voltage + (0.5 * SCALE) * drive[start : start + 8]
            voltage = jnp.where(bins == step, -0.5, voltage)
        out_ref[half, :, 0, 0] = jnp.where(live, voltage, 0.0)


def field_kernel(
    s_ref, rim_ref, init_ref, g_ref, ff_ref,
    cx_ref, sbuf, rbuf, rq_ref, iq_ref, tl_ref, til_ref, ro_ref, rh_ref, io_ref, ih_ref, p_ref, mb_ref,
    own_ref, hal_ref, inj_ref, cf_ref, hist_ref, mb2_ref, h2_ref, t_ref, ffs_ref, ffr_ref,
    cx_send, cx_recv, ring_send, ring_recv, q_send, q_recv, r2_send, r2_recv, a_send, a_recv,
    b_send, b_recv, f_send, f_recv, ag_send, ag_recv, ac_send, ac_recv,
):
    s = lax.axis_index("surf")
    g = lax.axis_index("neur")
    z = s // 4
    yh = (s // 2) % 2
    c = s % 2
    dzh = 2 * yh - 1

    def dev(zz, yy, cc, gg):
        return {"surf": lax.rem(zz + 16, 8) * 4 + yy * 2 + cc, "neur": gg}

    def rdma(src, dst, ss, rs, target):
        return pltpu.make_async_remote_copy(
            src_ref=src, dst_ref=dst, send_sem=ss, recv_sem=rs, device_id=target, device_id_type=pl.DeviceIdType.MESH
        )

    def zmod(dz):
        return lax.rem(z + dz + 16, 8)

    def gmod(i):
        return lax.rem(g + i, 8)

    barrier = pltpu.get_barrier_semaphore()
    me = (yh * 2 + c) * 8 + g

    def greet_plane(i, carry):
        other = lax.rem(me + i, 32)
        pl.semaphore_signal(
            barrier, inc=1, device_id=dev(z, other // 16, (other // 8) % 2, other % 8), device_id_type=pl.DeviceIdType.MESH
        )
        return carry

    lax.fori_loop(1, 32, greet_plane, 0)

    def greet_near(i, carry):
        pl.semaphore_signal(
            barrier, inc=1, device_id=dev(z + dzh, i // 8, c, i % 8), device_id_type=pl.DeviceIdType.MESH
        )
        return carry

    lax.fori_loop(0, 16, greet_near, 0)
    pl.semaphore_signal(barrier, inc=1, device_id=dev(z - dzh, yh, c, g), device_id_type=pl.DeviceIdType.MESH)
    pl.semaphore_wait(barrier, 31 + 17)

    partner = dev(z, yh, 1 - c, g)
    order = (4, 3, 5, 2, 6, 1, 7, 0)
    cx = {}
    for dz in order:
        cx[dz] = rdma(s_ref.at[zmod(dz), 1 - c], cx_ref.at[zmod(dz)], cx_send.at[dz], cx_recv.at[dz], partner)
        cx[dz].start()

    q = yh * 2 + c
    quad = []
    for i in range(1, 4):
        y2 = lax.rem(yh + i // 2, 2)
        c2 = lax.rem(c + i % 2, 2)
        target = dev(z, y2, c2, g)
        quad.append((y2 * 2 + c2, rdma(rim_ref, rq_ref.at[q], q_send.at[i], q_recv.at[q], target)))
        quad.append((y2 * 2 + c2, rdma(init_ref.at[pl.ds(c2 * 8, 8)], iq_ref.at[q], q_send.at[4 + i], q_recv.at[4 + q], target)))
    for _, copy in quad:
        copy.start()
    rq_ref[q] = rim_ref[...]
    iq_ref[q] = init_ref[pl.ds(c * 8, 8)]

    def x_of(dz, half):
        zd = zmod(dz)
        return s_ref[zd, c, half * 4 : half * 4 + 4].astype(F32) + cx_ref[zd, half * 4 : half * 4 + 4].astype(F32)

    ring = {}

    def ring_step(slot):
        letter, k = slot
        for way, sign in ((0, 1), (1, -1)):
            half = way if letter == "A" else 1 - way
            dz = sign * (4 - k)
            index = k if letter == "A" else 3 + k
            value = x_of(dz, half)
            first = k == (0 if letter == "A" else 1)
            if not first:
                ring[(way, index - 1)].wait_recv()
                value = value + rbuf[way, index - 1].astype(F32)
            sbuf[way, index] = value.astype(BF16)
            copy = rdma(
                sbuf.at[way, index], rbuf.at[way, index], ring_send.at[way, index], ring_recv.at[way, index],
                dev(z + sign, yh, c, g),
            )
            copy.start()
            ring[(way, index)] = copy

    cx[4].wait_recv()
    ring_step(("A", 0))
    cx[3].wait_recv()
    cx[5].wait_recv()
    ring_step(("B", 1))

    lane = lax.broadcasted_iota(jnp.int32, (8, LANES), 1)
    for i in range(1, 4):
        y2 = lax.rem(yh + i // 2, 2)
        c2 = lax.rem(c + i % 2, 2)
        src = y2 * 2 + c2
        rdma(rim_ref, rq_ref.at[src], q_send.at[i], q_recv.at[src], partner).wait_recv()
        rdma(init_ref.at[pl.ds(0, 8)], iq_ref.at[src], q_send.at[4 + i], q_recv.at[4 + src], partner).wait_recv()
    block = lane // 32
    for k in range(12):
        tl_ref[k] = jnp.where(
            block < 2,
            jnp.where(block == 0, rq_ref[0, k], rq_ref[1, k]),
            jnp.where(block == 2, rq_ref[2, k], rq_ref[3, k]),
        )
    for k in range(8):
        til_ref[k] = jnp.where(
            block < 2,
            jnp.where(block == 0, iq_ref[0, k], iq_ref[1, k]),
            jnp.where(block == 2, iq_ref[2, k], iq_ref[3, k]),
        )

    def setup_own(i):
        gg = gmod(i)
        target = dev(z, yh, c, gg)
        return (
            rdma(tl_ref, ro_ref.at[g], r2_send.at[0, i], r2_recv.at[0, g], target),
            rdma(til_ref.at[gg], io_ref.at[g], r2_send.at[1, i], r2_recv.at[1, g], target),
        )

    def setup_near(i):
        gg = gmod(i)
        target = dev(z - dzh, yh, c, gg)
        return (
            rdma(tl_ref, rh_ref.at[g], r2_send.at[2, i], r2_recv.at[2, g], target),
            rdma(til_ref.at[gg], ih_ref.at[g], r2_send.at[3, i], r2_recv.at[3, g], target),
        )

    def start_all(make):
        def body(i, carry):
            for copy in make(i):
                copy.start()
            return carry

        return body

    def sent_all(make):
        def body(i, carry):
            for copy in make(i):
                copy.wait_send()
            return carry

        return body

    lax.fori_loop(1, 8, start_all(setup_own), 0)
    lax.fori_loop(0, 8, start_all(setup_near), 0)
    ro_ref[g] = tl_ref[...]
    io_ref[g] = til_ref[g]

    cx[2].wait_recv()
    cx[6].wait_recv()
    ring_step(("A", 1))
    ring_step(("B", 2))
    ring_step(("A", 2))
    cx[1].wait_recv()
    cx[7].wait_recv()
    cx[0].wait_recv()
    ring_step(("B", 3))

    def setup_arrived(i, carry):
        gg = gmod(i)

        @pl.when(i > 0)
        def _():
            rdma(tl_ref, ro_ref.at[gg], r2_send.at[0, i], r2_recv.at[0, gg], partner).wait_recv()
            rdma(til_ref.at[0], io_ref.at[gg], r2_send.at[1, i], r2_recv.at[1, gg], partner).wait_recv()

        rdma(tl_ref, rh_ref.at[gg], r2_send.at[2, i], r2_recv.at[2, gg], partner).wait_recv()
        rdma(til_ref.at[0], ih_ref.at[gg], r2_send.at[3, i], r2_recv.at[3, gg], partner).wait_recv()
        return carry

    lax.fori_loop(0, 8, setup_arrived, 0)
    mine = (lane >= 32 * yh) & (lane < 96 + 32 * yh)
    row8 = lax.broadcasted_iota(jnp.int32, (8, LANES), 0)

    def couple(gg, carry):
        weights = [jnp.where(mine, ro_ref[gg, k], rh_ref[gg, k]) for k in range(6)]
        codes = [jnp.where(mine, ro_ref[gg, 6 + k], rh_ref[gg, 6 + k]) for k in range(6)]
        rows = pl.ds(pl.multiple_of(gg * 8, 8), 8)
        region = gg * 8 + row8
        for a in range(-RIM, RIM + 1):
            inside = (region + a >= 0) & (region + a < 64)
            for b in range(-RIM, RIM + 1):
                code = (a + RIM) * (2 * RIM + 1) + b + RIM
                if a == 0 and b == 0:
                    cf_ref[code, rows] = 0.9 - 0.15 * (weights[0] + weights[1] + weights[2] + weights[3] + weights[4] + weights[5])
                    continue
                total = jnp.zeros((8, LANES), F32)
                for k in range(6):
                    total = total + jnp.where(codes[k] == float(code), weights[k], 0.0)
                cf_ref[code, rows] = jnp.where(inside, 0.15 * total, 0.0)
        ffs_ref[rows] = jnp.where(mine, io_ref[gg], ih_ref[gg])
        return carry

    lax.fori_loop(0, 8, couple, 0)
    for a in range(-RIM, RIM + 1):
        if a != 0:
            for b in range(2 * RIM + 1):
                code = (a + RIM) * (2 * RIM + 1) + b
                cf_ref[code] = pltpu.roll(cf_ref[code], a % 64, 0)

    ring_step(("A", 3))

    for half in range(2):
        value = x_of(0, half)
        for way in range(2):
            index = 3 if way == half else 6
            ring[(way, index)].wait_recv()
            value = value + rbuf[way, index].astype(F32)
        p_ref[half * 320 : half * 320 + 320, :] = value.reshape(320, LANES)

    for n in range(8):
        for pair in range(STEPS // 2):
            parts = [p_ref[pl.ds((2 * pair + j) * 8 + n, 8, stride=ROWS), :] for j in range(2)]
            mb_ref[n, pair * 16 : pair * 16 + 16] = jnp.concatenate(parts, axis=0).astype(BF16)
    slot = yh * 8 + g

    def trial_own(k):
        n = gmod(k % 8)
        return (rdma(mb_ref.at[n], own_ref.at[slot], a_send.at[0, k], a_recv.at[0, slot], dev(z, lax.rem(yh + k // 8, 2), c, n)),)

    def trial_near(k):
        n = gmod(k % 8)
        up = k // 8
        return (rdma(mb_ref.at[n], hal_ref.at[slot], a_send.at[1, k], a_recv.at[1, slot], dev(z + 1 - 2 * up, up, c, n)),)

    lax.fori_loop(1, 16, start_all(trial_own), 0)
    lax.fori_loop(0, 16, start_all(trial_near), 0)
    own_ref[slot] = mb_ref[g]

    def trial_arrived(k, carry):
        @pl.when(k != slot)
        def _():
            rdma(mb_ref.at[0], own_ref.at[k], a_send.at[0, 0], a_recv.at[0, k], partner).wait_recv()

        rdma(mb_ref.at[0], hal_ref.at[k], a_send.at[1, 0], a_recv.at[1, k], partner).wait_recv()
        return carry

    lax.fori_loop(0, 16, trial_arrived, 0)
    lane16 = lax.broadcasted_iota(jnp.int32, (16, LANES), 1)
    mine16 = (lane16 >= 32 * yh) & (lane16 < 96 + 32 * yh)

    def unpack(gg, carry):
        rows = pl.ds(pl.multiple_of(gg * 8, 8), 8)
        for pair in range(STEPS // 2):
            tile = slice(pair * 16, pair * 16 + 16)
            value = jnp.where(
                mine16,
                own_ref[gg, tile].astype(F32) + own_ref[8 + gg, tile].astype(F32),
                hal_ref[gg, tile].astype(F32) + hal_ref[8 + gg, tile].astype(F32),
            )
            inj_ref[2 * pair, rows] = value[:8]
            inj_ref[2 * pair + 1, rows] = value[8:]
        return carry

    lax.fori_loop(0, 8, unpack, 0)

    def advance(step, carry):
        field, rate = carry
        rate = DECAY * rate + inj_ref[step]
        total = 0.1 * rate
        shifted = [field if b == 0 else pltpu.roll(field, (-b) % LANES, 1) for b in range(-RIM, RIM + 1)]
        for a in range(-RIM, RIM + 1):
            term = None
            for b in range(2 * RIM + 1):
                product = cf_ref[(a + RIM) * (2 * RIM + 1) + b] * shifted[b]
                term = product if term is None else term + product
            total = total + (term if a == 0 else pltpu.roll(term, (-a) % 64, 0))
        hist_ref[step] = total
        return (total, rate)

    last, _ = lax.fori_loop(0, STEPS, advance, (ffs_ref[...], jnp.zeros((64, LANES), F32)))
    ffs_ref[...] = last

    def pack(gg, carry):
        rows = pl.ds(pl.multiple_of(gg * 8, 8), 8)
        for pair in range(STEPS // 2):
            mb2_ref[gg, pair * 16 : pair * 16 + 16] = jnp.concatenate(
                [hist_ref[2 * pair, rows], hist_ref[2 * pair + 1, rows]], axis=0
            ).astype(BF16)
        return carry

    lax.fori_loop(0, 8, pack, 0)

    def back(k):
        gg = gmod(k % 8)
        return (rdma(mb2_ref.at[gg], h2_ref.at[slot], b_send.at[k], b_recv.at[slot], dev(z, lax.rem(yh + k // 8, 2), c, gg)),)

    trial = c * 8 + g

    def final(k):
        gg = gmod(k % 8)
        rows = pl.ds(pl.multiple_of(gg * 8, 8), 8)
        return (rdma(ffs_ref.at[rows], ffr_ref.at[trial], f_send.at[k], f_recv.at[trial], dev(z, yh, lax.rem(c + k // 8, 2), gg)),)

    lax.fori_loop(1, 16, start_all(back), 0)
    lax.fori_loop(1, 16, start_all(final), 0)
    h2_ref[slot] = mb2_ref[g]
    ffr_ref[trial] = ffs_ref[pl.ds(pl.multiple_of(g * 8, 8), 8)]

    def back_arrived(k, carry):
        @pl.when(k != slot)
        def _():
            rdma(mb2_ref.at[0], h2_ref.at[k], b_send.at[0], b_recv.at[k], partner).wait_recv()

        return carry

    lax.fori_loop(0, 16, back_arrived, 0)
    for n in range(8):
        for pair in range(STEPS // 2):
            tile = slice(pair * 16, pair * 16 + 16)
            value = jnp.where(lane16 < 64, h2_ref[n, tile].astype(F32), h2_ref[8 + n, tile].astype(F32))
            t_ref[pl.ds(pair * 128 + n, 16, stride=8), :] = value
    for r in range(8):
        for pair in range(STEPS // 2):
            parts = [t_ref[(2 * pair + j) * 64 + r * 8 : (2 * pair + j) * 64 + r * 8 + 8, :] for j in range(2)]
            g_ref[z, c, r, pair * 16 : pair * 16 + 16] = jnp.concatenate(parts, axis=0).astype(BF16)

    ag = {}
    pieces = []

    def to_core(zz, half, index):
        piece = g_ref.at[zz, c, pl.ds(half * 4, 4)]
        copy = rdma(piece, piece, ac_send.at[index], ac_recv.at[index], partner)
        copy.start()
        pieces.append((zz, half, index, copy))

    def ag_step(slot_index, letter, k):
        for way, sign in ((0, 1), (1, -1)):
            half = way if letter == 0 else 1 - way
            zz = zmod(-sign * k)
            if k > 0:
                ag[(way, slot_index - 2)].wait_recv()
            piece = g_ref.at[zz, c, pl.ds(half * 4, 4)]
            copy = rdma(piece, piece, ag_send.at[way, slot_index], ag_recv.at[way, slot_index], dev(z + sign, yh, c, g))
            copy.start()
            ag[(way, slot_index)] = copy
            if k > 0:
                to_core(zz, half, way * 7 + slot_index - 2)

    for slot_index in range(7):
        ag_step(slot_index, slot_index % 2, slot_index // 2)
        if slot_index == 1:
            to_core(z, 0, 14)
            to_core(z, 1, 15)

    def final_arrived(k, carry):
        @pl.when(k != trial)
        def _():
            rdma(ffs_ref.at[pl.ds(0, 8)], ffr_ref.at[k], f_send.at[0], f_recv.at[k], partner).wait_recv()

        return carry

    lax.fori_loop(0, 16, final_arrived, 0)
    for k in range(16):
        value = pltpu.roll(ffr_ref[k], lax.rem(128 - 32 * q, 128), 1)
        ff_ref[k] = value[:, :32]

    for slot_index in (5, 6):
        for way, sign in ((0, 1), (1, -1)):
            ag[(way, slot_index)].wait_recv()
            letter, k = slot_index % 2, slot_index // 2
            half = way if letter == 0 else 1 - way
            to_core(zmod(-sign * (k + 1)), half, way * 7 + slot_index)
    for zz, half, index, copy in pieces:
        other = g_ref.at[zz, 1 - c, pl.ds(half * 4, 4)]
        rdma(other, other, ac_send.at[index], ac_recv.at[index], partner).wait_recv()

    for dz in order:
        cx[dz].wait_send()
    for _, copy in quad:
        copy.wait_send()
    for copy in ring.values():
        copy.wait_send()
    lax.fori_loop(1, 8, sent_all(setup_own), 0)
    lax.fori_loop(0, 8, sent_all(setup_near), 0)
    lax.fori_loop(1, 16, sent_all(trial_own), 0)
    lax.fori_loop(0, 16, sent_all(trial_near), 0)
    lax.fori_loop(1, 16, sent_all(back), 0)
    lax.fori_loop(1, 16, sent_all(final), 0)
    for copy in ag.values():
        copy.wait_send()
    for _, _, _, copy in pieces:
        copy.wait_send()


def local(spike_bins, neuron_site, efficacy, region_live, membrane_init, field_init, rim_weights, rim_codes):
    trials, regions, slots = spike_bins.shape
    bins5 = spike_bins.reshape(2, 8, regions, 1, slots)
    init5 = membrane_init.reshape(2, 8, regions, 1, slots)
    smem = pl.BlockSpec(memory_space=pltpu.SMEM)
    vmem = pl.BlockSpec(memory_space=pltpu.VMEM)
    row_block = pl.BlockSpec((2, 8, 1, 1, slots), lambda r: (0, 0, r, 0, 0))
    whole = pl.BlockSpec((regions, slots), lambda r: (0, 0))
    field_block = pl.BlockSpec((8, 2, 1, ROWS, LANES), lambda r: (0, 0, r, 0, 0))
    params = pltpu.CompilerParams(vmem_limit_bytes=VMEM_LIMIT)
    spread = pl.pallas_call(
        spread_kernel,
        grid=(regions,),
        out_shape=jax.ShapeDtypeStruct((8, 2, regions, ROWS, LANES), BF16),
        in_specs=[smem, row_block, whole, whole],
        out_specs=field_block,
        scratch_shapes=[pltpu.VMEM((1024, slots), BF16)],
        compiler_params=params,
        name="spread",
    )(region_live, bins5, neuron_site, efficacy.astype(F32))
    rim = jnp.tile(jnp.concatenate([rim_weights, rim_codes.astype(F32)], axis=0), (1, 1, 4))
    init = jnp.tile(field_init, (1, 1, 4))
    dma = pltpu.SemaphoreType.DMA
    gathered, field_final = pl.pallas_call(
        field_kernel,
        out_shape=(
            jax.ShapeDtypeStruct((8, 2, regions, ROWS, LANES), BF16),
            jax.ShapeDtypeStruct((16, 8, 32), F32),
        ),
        in_specs=[vmem, vmem, vmem],
        out_specs=(vmem, vmem),
        scratch_shapes=[
            pltpu.VMEM((8, 8, ROWS, LANES), BF16),
            pltpu.VMEM((2, 7, 4, ROWS, LANES), BF16),
            pltpu.VMEM((2, 7, 4, ROWS, LANES), BF16),
            pltpu.VMEM((4, 12, 8, LANES), F32),
            pltpu.VMEM((4, 8, 8, LANES), F32),
            pltpu.VMEM((12, 8, LANES), F32),
            pltpu.VMEM((8, 8, LANES), F32),
            pltpu.VMEM((8, 12, 8, LANES), F32),
            pltpu.VMEM((8, 12, 8, LANES), F32),
            pltpu.VMEM((8, 8, LANES), F32),
            pltpu.VMEM((8, 8, LANES), F32),
            pltpu.VMEM((640, LANES), F32),
            pltpu.VMEM((8, ROWS, LANES), BF16),
            pltpu.VMEM((16, ROWS, LANES), BF16),
            pltpu.VMEM((16, ROWS, LANES), BF16),
            pltpu.VMEM((STEPS, 64, LANES), F32),
            pltpu.VMEM((25, 64, LANES), F32),
            pltpu.VMEM((STEPS, 64, LANES), F32),
            pltpu.VMEM((8, ROWS, LANES), BF16),
            pltpu.VMEM((16, ROWS, LANES), BF16),
            pltpu.VMEM((640, LANES), F32),
            pltpu.VMEM((64, LANES), F32),
            pltpu.VMEM((16, 8, LANES), F32),
            dma((8,)), dma((8,)), dma((2, 7)), dma((2, 7)), dma((8,)), dma((8,)),
            dma((4, 8)), dma((4, 8)), dma((2, 16)), dma((2, 16)), dma((16,)), dma((16,)),
            dma((16,)), dma((16,)), dma((2, 7)), dma((2, 7)), dma((16,)), dma((16,)),
        ],
        compiler_params=pltpu.CompilerParams(vmem_limit_bytes=VMEM_LIMIT, collective_id=0, has_side_effects=True),
        name="field",
    )(spread, rim, init)
    membranes = pl.pallas_call(
        collect_kernel,
        grid=(regions,),
        out_shape=jax.ShapeDtypeStruct((2, 8, regions, 1, slots), F32),
        in_specs=[smem, field_block, row_block, whole, row_block],
        out_specs=row_block,
        scratch_shapes=[pltpu.VMEM((1024, slots), BF16)],
        compiler_params=params,
        name="collect",
    )(region_live, gathered, bins5, neuron_site, init5)
    return field_final, membranes.reshape(trials, regions, slots)


def solution(mesh):
    in_specs = (
        P(None, "neur", "surf"),
        P("neur", "surf"),
        P("neur", "surf"),
        P("neur"),
        P(None, "neur", "surf"),
        P(None, "neur", "surf"),
        P(None, "neur", "surf"),
        P(None, "neur", "surf"),
    )
    out_specs = (P(None, "neur", "surf"), P(None, "neur", "surf"))
    return jax.shard_map(local, mesh=mesh, in_specs=in_specs, out_specs=out_specs, check_vma=False)
```

time: 856 us -> 110 us (0.13)
  waiting for transfers between devices: 251 us -> 0 us
  matrix products: 243 us -> 0 us
  local copies, waits for them, and re-layouts: 166 us -> 8.13 us
  starting transfers between devices: 117 us -> 0 us
  Pallas kernels: 0 us -> 99.4 us
  other arithmetic: 57.4 us -> 1.35 us
  between operations: 14.2 us -> 0.7 us
    dot_general x16 -> x0, matrix products: 243 us -> none  [the longest x8 124 us: one_region(): jnp.dot(matrix, rows_region, precision=lax.Precision.HIGHEST, preferred_e...]
    unnamed x3 -> x0, waiting for transfers between devices: 120 us -> none
    ppermute x40 -> x0, starting transfers between devices: 117 us -> none  [the longest x20 84.2 us: padded(): after = lax.ppermute(leading, axis, down)]
    dynamic_update_slice x16 -> x0, local copies, waits for them, and re-layouts: 112 us -> none  [band_spreader(): by_region = lax.map(one_region, (site_ids, values))]
    pallas_call x0 -> x3, Pallas kernels: none -> 99.4 us  [the longest x1 81.9 us: local(): pl.pallas_call(field_kernel, out_shape=(jax.ShapeDtypeStruct((8, 2, regio...]
    all_gather x1 -> x0, waiting for transfers between devices: 84.4 us -> none  [local(): lax.all_gather(history_rows, 'surf', axis=0, tiled=True)]
    ppermute x40 -> x0, waiting for transfers between devices: 46.4 us -> none  [the longest x20 42.9 us: padded(): after = lax.ppermute(leading, axis, down)]
    select_n x11 -> x0, other arithmetic: 20.9 us -> none  [the longest x10 20.1 us: membrane_step(): jnp.where(spike_bins == step_index, -0.5 * jnp.ones_like(voltage), voltage)]
  transfers between devices with their start and end apart: 42 -> 0, of which waited for: 30 -> 0; matrix products, arithmetic and copies ran while one was open for 0% -> 0% of each run, Pallas kernels for 0% -> 0%
where the time goes in v1:
time: 110 us
  Pallas kernels  99.4 us (90%)
  local copies, waits for them, and re-layouts  8.13 us (7%)
  other arithmetic  1.35 us (1%)
    pallas_call x1, Pallas kernels, local(): pl.pallas_call(field_kernel, out_shape=(jax.ShapeDtypeStruct((8, 2, regio...  81.9 us
    pallas_call x1, Pallas kernels, local(): pl.pallas_call(spread_kernel, grid=(regions,), out_shape=jax.ShapeDtypeSt...  9.17 us
    pallas_call x1, Pallas kernels, local(): pl.pallas_call(collect_kernel, grid=(regions,), out_shape=jax.ShapeDtypeS...  8.35 us
    unnamed x12, local copies, waits for them, and re-layouts  2.58 us
    reshape x1, local copies, waits for them, and re-layouts, local(): bins5 = spike_bins.reshape(2, 8, regions, 1, slots)  2.48 us

profile of v1, /device:TPU:1, one launch (start us, length us, event | category | flops | bytes accessed | tf_op | source)
XLA Modules:
  0.0 109.6 jit_solution(11585002757746727067)
XLA Ops:
  0.6 0.0 copy-start.1
  0.6 0.0 copy-start.3
  0.7 0.0 copy-start.4
  0.7 2.5 %reshape.21.bins_ref = s32[2,8,8,1,1024]{4,3,2,1,0:T(1,128)} reshape(s32[16,8,1024]{2,1,0:T(8,128)} %param.8) | data formatting | bytes 1048576 | tf_op jit(solution)/shard_map/reshape | solution.py:480
  3.1 1.3 %convert_element_type.6.eff_ref = f32[8,1024]{1,0:T(8,128)} convert(bf16[8,1024]{1,0:T(8,128)(2,1)} %param.10) | non-fusion elementwise | flops 8192 | bytes 49152 | tf_op jit(solution)/shard_map/convert_element_type | solution.py:497
  4.5 9.2 %spread.1.s_ref = bf16[8,2,8,80,128]{4,3,2,1,0:T(8,128)(2,1)} custom-call(s32[8]{0:T(128)} %live_ref.3, s32[2,8,8,1,1024]{4,3,2,1,0:T(1,128)} %reshape.21.bins_ref, s32[8,1024]{1,0:T(8,128)} %site_ref.3, f32[8,1024]{1,0:T(8,128)} %convert_element_type.6.eff_ref), custom_call_target="tpu_custom_call" | custom-call | tf_op jit(solution)/shard_map/spread/pallas_call | solution.py:488
  13.6 0.0 copy-done.1
  13.6 0.0 copy-start
  13.7 0.1 tile.20
  13.7 0.8 tile.21.init_ref
  14.5 0.0 copy-done.3
  14.5 0.0 copy-done.4
  14.6 0.8 tile.9.rim_ref
  15.3 81.9 %field.1 = (bf16[8,2,8,80,128]{4,3,2,1,0:T(8,128)(2,1)}, f32[16,8,32]{2,1,0:T(8,128)}) custom-call(bf16[8,2,8,80,128]{4,3,2,1,0:T(8,128)(2,1)} %spread.1.s_ref, f32[12,8,128]{2,1,0:T(8,128)} %tile.9.rim_ref, f32[16,8,128]{2,1,0:T(8,128)} %tile.21.init_ref), custom_call_target="tpu_custom_call" | custom-call | tf_op jit(solution)/shard_map/field/pallas_call | solution.py:501
  97.3 0.0 copy-done
  97.3 1.4 %reshape.22.init_ref = f32[2,8,8,1,1024]{4,3,2,1,0:T(1,128)} reshape(f32[16,8,1024]{2,1,0:T(8,128)S(1)} %copy-done) | data formatting | bytes 1048576 | tf_op jit(solution)/shard_map/reshape | solution.py:481
  98.7 0.0 copy-start.2
  98.7 8.3 %collect.1 = f32[2,8,8,1,1024]{4,3,2,1,0:T(1,128)} custom-call(s32[8]{0:T(128)} %live_ref.3, bf16[8,2,8,80,128]{4,3,2,1,0:T(8,128)(2,1)} %get-tuple-element.5.gather_ref, s32[2,8,8,1,1024]{4,3,2,1,0:T(1,128)} %reshape.21.bins_ref, s32[8,1024]{1,0:T(8,128)} %site_ref.3, f32[2,8,8,1,1024]{4,3,2,1,0:T(1,128)} %reshape.22.init_ref), custom_call_target="tpu_custom_call" | custom-call | tf_op jit(solution)/shard_map/collect/pallas_call | solution.py:540
  107.1 1.9 %copy.10 = f32[2,8,8,1,1024]{4,2,3,1,0:T(8,128)} copy(f32[2,8,8,1,1024]{4,3,2,1,0:T(1,128)} %collect.1) | data formatting | bytes 1048576
  109.0 0.0 copy-done.2
  109.0 0.6 copy.12
  (3 shorter events, 0.1 us)
Async XLA Ops:
  0.6 13.0 %copy-start.1 = (f32[16,8,32]{2,1,0:T(8,128)S(1)}, f32[16,8,32]{2,1,0:T(8,128)}, u32[]{:S(2)}) copy-start(f32[16,8,32]{2,1,0:T(8,128)} %param.13) | copy-start | bytes 49156
  0.6 13.9 %copy-start.3 = (s32[6,8,32]{2,1,0:T(8,128)S(1)}, s32[6,8,32]{2,1,0:T(8,128)}, u32[]{:S(2)}) copy-start(s32[6,8,32]{2,1,0:T(8,128)} %param.15) | copy-start | bytes 18436
  0.7 13.9 %copy-start.4 = (f32[6,8,32]{2,1,0:T(8,128)S(1)}, f32[6,8,32]{2,1,0:T(8,128)}, u32[]{:S(2)}) copy-start(f32[6,8,32]{2,1,0:T(8,128)} %param.14) | copy-start | bytes 18436
  13.6 83.6 %copy-start = (f32[16,8,1024]{2,1,0:T(8,128)S(1)}, f32[16,8,1024]{2,1,0:T(8,128)}, u32[]{:S(2)}) copy-start(f32[16,8,1024]{2,1,0:T(8,128)} %param.12) | copy-start | bytes 1572868
  98.7 10.3 %copy-start.2 = (f32[16,8,32]{2,1,0:T(8,128)S(1)}, f32[16,8,32]{2,1,0:T(8,128)}, u32[]{:S(2)}) copy-start(f32[16,8,32]{2,1,0:T(8,128)} %get-tuple-element.8) | copy-start | bytes 49156

commit v2 on v1

v2 whole, which is shorter than its diff:
```python
import math

import jax
import jax.numpy as jnp
from jax import lax
from jax.experimental import pallas as pl
from jax.experimental.pallas import tpu as pltpu
from jax.sharding import PartitionSpec as P

STEPS = 10
RIM = 2
FOOT = 8
TAPS = (0.84375, 0.51171875, 0.310546875, 0.1884765625, 0.1142578125, 0.0693359375, 0.0419921875, 0.025390625)
SCALE = 1.0 / sum(TAPS)
DECAY = math.exp(-0.35)
F32 = jnp.float32
BF16 = jnp.bfloat16
VMEM_LIMIT = 56 * 1024 * 1024
ROWS = 80
LANES = 128


def build_band(site, band_ref):
    total, slots = band_ref.shape[-2:]
    tiles = total // 16
    high = jnp.broadcast_to((site >> 4).astype(F32).astype(BF16), (16, slots))
    low = jnp.broadcast_to(site & 15, (16, slots))
    row = lax.broadcasted_iota(jnp.int32, (16, slots), 0)
    first = jnp.zeros((16, slots), F32)
    second = jnp.zeros((16, slots), F32)
    for offset in range(FOOT):
        first = jnp.where(row - low == offset, TAPS[offset], first)
        second = jnp.where(row + 16 - low == offset, TAPS[offset], second)
    first, second = first.astype(BF16), second.astype(BF16)
    zero = jnp.zeros((16, slots), BF16)
    for tile in range(tiles):
        here = high == jnp.asarray(tile, BF16)
        before = high == jnp.asarray((tile - 1) % tiles, BF16)
        band_ref[tile * 16 : tile * 16 + 16, :] = jnp.where(here, first, jnp.where(before, second, zero))


def fused_kernel(
    live_ref, bins_ref, site_ref, eff_ref, start_ref, field_ref, weights_ref, codes_ref,
    ff_ref, out_ref,
    weff_ref, tbins_ref, tstart_ref, band_ref, charge_ref, drive_ref, s_ref, g_ref, rim_ref, init_ref,
    cx_ref, sbuf, rbuf, rq_ref, iq_ref, tl_ref, til_ref, th_ref, tih_ref, tm_ref, tim_ref, ro_ref, io_ref, p_ref, mb_ref, mh_ref,
    own_ref, hal_ref, inj_ref, cf_ref, hist_ref, mb2_ref, h2_ref, t_ref, ffs_ref, ffr_ref,
    cx_send, cx_recv, ring_send, ring_recv, q_send, q_recv, n_send, n_recv, r2_send, r2_recv, a_send, a_recv,
    b_send, b_recv, f_send, f_recv, ag_send, ag_recv, ay_send, ay_recv, ac_send, ac_recv,
):
    s = lax.axis_index("surf")
    g = lax.axis_index("neur")
    z = s // 4
    yh = (s // 2) % 2
    c = s % 2
    dzh = 2 * yh - 1

    def dev(zz, yy, cc, gg):
        return {"surf": lax.rem(zz + 16, 8) * 4 + yy * 2 + cc, "neur": gg}

    def rdma(src, dst, ss, rs, target):
        return pltpu.make_async_remote_copy(
            src_ref=src, dst_ref=dst, send_sem=ss, recv_sem=rs, device_id=target, device_id_type=pl.DeviceIdType.MESH
        )

    def zmod(dz):
        return lax.rem(z + dz + 16, 8)

    def gmod(i):
        return lax.rem(g + i, 8)

    barrier = pltpu.get_barrier_semaphore()
    me = (yh * 2 + c) * 8 + g

    def greet_plane(i, carry):
        other = lax.rem(me + i, 32)
        pl.semaphore_signal(
            barrier, inc=1, device_id=dev(z, other // 16, (other // 8) % 2, other % 8), device_id_type=pl.DeviceIdType.MESH
        )
        return carry

    lax.fori_loop(1, 32, greet_plane, 0)

    def greet_near(i, carry):
        pl.semaphore_signal(
            barrier, inc=1, device_id=dev(z + dzh, i // 8, c, i % 8), device_id_type=pl.DeviceIdType.MESH
        )
        return carry

    lax.fori_loop(0, 16, greet_near, 0)
    pl.semaphore_signal(barrier, inc=1, device_id=dev(z - dzh, yh, c, g), device_id_type=pl.DeviceIdType.MESH)

    slots = site_ref.shape[1]
    slot_id = s * slots + lax.broadcasted_iota(jnp.int32, (1, slots), 1)

    for tile in range(8):
        tbins_ref[tile * 128 : tile * 128 + 128, :] = bins_ref[:, tile * LANES : tile * LANES + LANES]
        tstart_ref[tile * 128 : tile * 128 + 128, :] = start_ref[:, tile * LANES : tile * LANES + LANES]

    weff_ref[...] = eff_ref[...].astype(F32)

    def trials_of(ref, half, region):
        first = half * 64 + region
        return jnp.concatenate([ref[pl.ds(tile * 128 + first, 8, stride=8), :] for tile in range(8)], axis=1)

    def spread(region, carry):
        weight = jnp.where(slot_id < live_ref[region], weff_ref[pl.ds(region, 1), :], 0.0)
        weight = jnp.broadcast_to(weight, (8, slots))
        band = band_ref.at[region]
        build_band(site_ref[pl.ds(region, 1), :], band)
        for half in range(2):
            bins = trials_of(tbins_ref, half, region)
            for pair in range(STEPS // 2):
                rows = [jnp.where(bins == 2 * pair + j, weight, 0.0) for j in range(2)]
                start = half * ROWS + pair * 16
                charge_ref[start : start + 16, :] = jnp.concatenate(rows, axis=0).astype(BF16)
        total = lax.dot_general(charge_ref[...], band[...], (((1,), (1,)), ((), ())), preferred_element_type=F32)
        total = (total * SCALE).astype(BF16)
        for plane in range(8):
            for half in range(2):
                s_ref[plane, half, region] = total[half * ROWS : half * ROWS + ROWS, plane * LANES : plane * LANES + LANES]
        return carry

    partner = dev(z, yh, 1 - c, g)
    cx = {}

    def quarter(index):
        lax.fori_loop(2 * index, 2 * index + 2, spread, 0)

    def to_partner(index):
        part = pl.ds(2 * index, 2)
        cx[index] = rdma(s_ref.at[:, 1 - c, part], cx_ref.at[:, part], cx_send.at[index], cx_recv.at[index], partner)
        cx[index].start()

    quarter(0)
    pl.semaphore_wait(barrier, 31 + 17)
    to_partner(0)

    q = yh * 2 + c
    for k in range(6):
        rim_ref[k] = jnp.concatenate([weights_ref[k]] * 4, axis=1)
        rim_ref[6 + k] = jnp.concatenate([codes_ref[k].astype(F32)] * 4, axis=1)
    for k in range(16):
        init_ref[k] = jnp.concatenate([field_ref[k]] * 4, axis=1)
    quad = []
    for i in range(1, 4):
        y2 = lax.rem(yh + i // 2, 2)
        c2 = lax.rem(c + i % 2, 2)
        target = dev(z, y2, c2, g)
        quad.append((y2 * 2 + c2, rdma(rim_ref, rq_ref.at[q], q_send.at[i], q_recv.at[q], target)))
        quad.append((y2 * 2 + c2, rdma(init_ref.at[pl.ds(c2 * 8, 8)], iq_ref.at[q], q_send.at[4 + i], q_recv.at[4 + q], target)))
    for _, copy in quad:
        copy.start()
    rq_ref[q] = rim_ref[...]
    iq_ref[q] = init_ref[pl.ds(c * 8, 8)]


    def x_of(dz, index):
        zd = zmod(dz)
        part = slice(2 * index, 2 * index + 2)
        return s_ref[zd, c, part].astype(F32) + cx_ref[zd, part].astype(F32)

    ring = {}

    def hop(index, k):
        for way, sign in ((0, 1), (1, -1)):
            first = 4 if way == index % 2 else 3
            if k >= first:
                continue
            value = x_of(sign * (first - k), index)
            if k == 0:
                pass
            else:
                ring[(way, index, k - 1)].wait_recv()
                value = value + rbuf[way, index, k - 1].astype(F32)
            sbuf[way, index, k] = value.astype(BF16)
            copy = rdma(
                sbuf.at[way, index, k], rbuf.at[way, index, k], ring_send.at[way, index, k], ring_recv.at[way, index, k],
                dev(z + sign, yh, c, g),
            )
            copy.start()
            ring[(way, index, k)] = copy

    quarter(1)
    to_partner(1)
    cx[0].wait_recv()
    hop(0, 0)
    quarter(2)
    to_partner(2)
    cx[1].wait_recv()
    hop(1, 0)
    hop(0, 1)
    quarter(3)
    to_partner(3)
    cx[2].wait_recv()
    hop(2, 0)
    hop(1, 1)
    hop(0, 2)

    lane = lax.broadcasted_iota(jnp.int32, (8, LANES), 1)
    for i in range(1, 4):
        y2 = lax.rem(yh + i // 2, 2)
        c2 = lax.rem(c + i % 2, 2)
        src = y2 * 2 + c2
        rdma(rim_ref, rq_ref.at[src], q_send.at[i], q_recv.at[src], partner).wait_recv()
        rdma(init_ref.at[pl.ds(0, 8)], iq_ref.at[src], q_send.at[4 + i], q_recv.at[4 + src], partner).wait_recv()
    block = lane // 32
    for k in range(12):
        tl_ref[k] = jnp.where(
            block < 2,
            jnp.where(block == 0, rq_ref[0, k], rq_ref[1, k]),
            jnp.where(block == 2, rq_ref[2, k], rq_ref[3, k]),
        )
    for k in range(8):
        til_ref[k] = jnp.where(
            block < 2,
            jnp.where(block == 0, iq_ref[0, k], iq_ref[1, k]),
            jnp.where(block == 2, iq_ref[2, k], iq_ref[3, k]),
        )

    near = (
        rdma(tl_ref, th_ref, n_send.at[0], n_recv.at[0], dev(z - dzh, yh, c, g)),
        rdma(til_ref, tih_ref, n_send.at[1], n_recv.at[1], dev(z - dzh, yh, c, g)),
    )
    for copy in near:
        copy.start()

    def setup_own(i):
        gg = gmod(i)
        target = dev(z, yh, c, gg)
        return (
            rdma(tm_ref, ro_ref.at[g], r2_send.at[0, i], r2_recv.at[0, g], target),
            rdma(tim_ref.at[gg], io_ref.at[g], r2_send.at[1, i], r2_recv.at[1, g], target),
        )

    def start_all(make):
        def body(i, carry):
            for copy in make(i):
                copy.start()
            return carry

        return body

    def sent_all(make):
        def body(i, carry):
            for copy in make(i):
                copy.wait_send()
            return carry

        return body

    cx[3].wait_recv()
    hop(3, 0)
    hop(2, 1)
    hop(1, 2)

    mine = (lane >= 32 * yh) & (lane < 96 + 32 * yh)
    for copy in near:
        copy.wait_recv()
    for k in range(12):
        tm_ref[k] = jnp.where(mine, tl_ref[k], th_ref[k])
    for k in range(8):
        tim_ref[k] = jnp.where(mine, til_ref[k], tih_ref[k])
    lax.fori_loop(1, 8, start_all(setup_own), 0)
    ro_ref[g] = tm_ref[...]
    io_ref[g] = tim_ref[g]

    hop(0, 3)
    hop(3, 1)
    hop(2, 2)

    def setup_arrived(i, carry):
        gg = gmod(i)
        rdma(tm_ref, ro_ref.at[gg], r2_send.at[0, i], r2_recv.at[0, gg], partner).wait_recv()
        rdma(tim_ref.at[0], io_ref.at[gg], r2_send.at[1, i], r2_recv.at[1, gg], partner).wait_recv()
        return carry

    lax.fori_loop(1, 8, setup_arrived, 0)
    row8 = lax.broadcasted_iota(jnp.int32, (8, LANES), 0)

    def couple(gg, carry):
        weights = [ro_ref[gg, k] for k in range(6)]
        codes = [ro_ref[gg, 6 + k] for k in range(6)]
        rows = pl.ds(pl.multiple_of(gg * 8, 8), 8)
        region = gg * 8 + row8
        for a in range(-RIM, RIM + 1):
            inside = (region + a >= 0) & (region + a < 64)
            for b in range(-RIM, RIM + 1):
                code = (a + RIM) * (2 * RIM + 1) + b + RIM
                if a == 0 and b == 0:
                    cf_ref[code, rows] = 0.9 - 0.15 * (weights[0] + weights[1] + weights[2] + weights[3] + weights[4] + weights[5])
                    continue
                total = jnp.zeros((8, LANES), F32)
                for k in range(6):
                    total = total + jnp.where(codes[k] == float(code), weights[k], 0.0)
                cf_ref[code, rows] = jnp.where(inside, 0.15 * total, 0.0)
        ffs_ref[rows] = io_ref[gg]
        return carry

    lax.fori_loop(0, 8, couple, 0)
    for a in range(-RIM, RIM + 1):
        if a != 0:
            for b in range(2 * RIM + 1):
                code = (a + RIM) * (2 * RIM + 1) + b
                cf_ref[code] = pltpu.roll(cf_ref[code], a % 64, 0)

    hop(1, 3)
    hop(3, 2)
    hop(2, 3)
    hop(3, 3)

    for index in range(4):
        value = x_of(0, index)
        for way in range(2):
            k = 3 if way == index % 2 else 2
            ring[(way, index, k)].wait_recv()
            value = value + rbuf[way, index, k].astype(F32)
        p_ref[index * 160 : index * 160 + 160, :] = value.reshape(160, LANES)

    lane16 = lax.broadcasted_iota(jnp.int32, (16, LANES), 1)
    block16 = lane16 // 32

    def by_block(tiles):
        return jnp.where(
            block16 < 2, jnp.where(block16 == 0, tiles[0], tiles[1]), jnp.where(block16 == 2, tiles[2], tiles[3])
        )

    for n in range(8):
        tiles = []
        for pair in range(STEPS // 2):
            parts = [p_ref[pl.ds((2 * pair + j) * 8 + n, 8, stride=ROWS), :] for j in range(2)]
            tiles.append(jnp.concatenate(parts, axis=0))
            mb_ref[n, pair * 16 : pair * 16 + 16] = tiles[-1].astype(BF16)
        high = [pltpu.roll(tiles[j], 32 * j + 32, 1) if j < 3 else tiles[j] for j in range(4)]
        low = [pltpu.roll(tiles[j], 32 * j, 1) if j > 0 else tiles[j] for j in range(4)]
        mh_ref[0, n, :16] = by_block(high).astype(BF16)
        mh_ref[1, n, :16] = by_block(low).astype(BF16)
        mh_ref[0, n, 16:] = tiles[4].astype(BF16)
        mh_ref[1, n, 16:] = tiles[4].astype(BF16)
    slot = yh * 8 + g

    def trial_own(k):
        n = gmod(k % 8)
        return (rdma(mb_ref.at[n], own_ref.at[slot], a_send.at[0, k], a_recv.at[0, slot], dev(z, lax.rem(yh + k // 8, 2), c, n)),)

    def trial_near(k):
        n = gmod(k % 8)
        up = k // 8
        return (rdma(mh_ref.at[up, n], hal_ref.at[slot], a_send.at[1, k], a_recv.at[1, slot], dev(z + 1 - 2 * up, up, c, n)),)

    lax.fori_loop(1, 16, start_all(trial_own), 0)
    lax.fori_loop(0, 16, start_all(trial_near), 0)
    own_ref[slot] = mb_ref[g]

    def trial_arrived(k, carry):
        @pl.when(k != slot)
        def _():
            rdma(mb_ref.at[0], own_ref.at[k], a_send.at[0, 0], a_recv.at[0, k], partner).wait_recv()

        rdma(mh_ref.at[0, 0], hal_ref.at[k], a_send.at[1, 0], a_recv.at[1, k], partner).wait_recv()
        return carry

    lax.fori_loop(0, 16, trial_arrived, 0)
    mine16 = (lane16 >= 32 * yh) & (lane16 < 96 + 32 * yh)

    def unpack(gg, carry):
        rows = pl.ds(pl.multiple_of(gg * 8, 8), 8)
        edge = hal_ref[gg].astype(F32) + hal_ref[8 + gg].astype(F32)
        for pair in range(STEPS // 2):
            tile = slice(pair * 16, pair * 16 + 16)
            near_edge = pltpu.roll(edge[:16], lax.rem(96 * (1 - yh) - 32 * pair + 128, 128), 1) if pair < 4 else edge[16:]
            value = jnp.where(mine16, own_ref[gg, tile].astype(F32) + own_ref[8 + gg, tile].astype(F32), near_edge)
            inj_ref[2 * pair, rows] = value[:8]
            inj_ref[2 * pair + 1, rows] = value[8:]
        return carry

    lax.fori_loop(0, 8, unpack, 0)

    def advance(step, carry):
        field, rate = carry
        rate = DECAY * rate + inj_ref[step]
        total = 0.1 * rate
        shifted = [field if b == 0 else pltpu.roll(field, (-b) % LANES, 1) for b in range(-RIM, RIM + 1)]
        for a in range(-RIM, RIM + 1):
            term = None
            for b in range(2 * RIM + 1):
                product = cf_ref[(a + RIM) * (2 * RIM + 1) + b] * shifted[b]
                term = product if term is None else term + product
            total = total + (term if a == 0 else pltpu.roll(term, (-a) % 64, 0))
        hist_ref[step] = total
        return (total, rate)

    last, _ = lax.fori_loop(0, STEPS, advance, (ffs_ref[...], jnp.zeros((64, LANES), F32)))
    ffs_ref[...] = last

    mine64 = (lane16 >= 64 * yh) & (lane16 < 64 + 64 * yh)

    def pack(gg, carry):
        rows = pl.ds(pl.multiple_of(gg * 8, 8), 8)
        tiles = [
            jnp.concatenate([hist_ref[2 * pair, rows], hist_ref[2 * pair + 1, rows]], axis=0) for pair in range(STEPS // 2)
        ]
        for m in range(2):
            both = jnp.where(mine64, tiles[2 * m], pltpu.roll(tiles[2 * m + 1], 64, 1))
            mb2_ref[gg, m * 16 : m * 16 + 16] = both.astype(BF16)
        mb2_ref[gg, 32:48] = tiles[4].astype(BF16)
        return carry

    lax.fori_loop(0, 8, pack, 0)

    def back(k):
        gg = gmod(k % 8)
        return (rdma(mb2_ref.at[gg], h2_ref.at[slot], b_send.at[k], b_recv.at[slot], dev(z, lax.rem(yh + k // 8, 2), c, gg)),)

    trial = c * 8 + g

    def final(k):
        gg = gmod(k % 8)
        rows = pl.ds(pl.multiple_of(gg * 8, 8), 8)
        return (rdma(ffs_ref.at[rows], ffr_ref.at[trial], f_send.at[k], f_recv.at[trial], dev(z, yh, lax.rem(c + k // 8, 2), gg)),)

    lax.fori_loop(1, 16, start_all(back), 0)
    lax.fori_loop(1, 16, start_all(final), 0)
    h2_ref[slot] = mb2_ref[g]
    ffr_ref[trial] = ffs_ref[pl.ds(pl.multiple_of(g * 8, 8), 8)]

    def back_arrived(k, carry):
        @pl.when(k != slot)
        def _():
            rdma(mb2_ref.at[0], h2_ref.at[k], b_send.at[0], b_recv.at[k], partner).wait_recv()

        return carry

    lax.fori_loop(0, 16, back_arrived, 0)
    for n in range(8):
        for m in range(3):
            tile = slice(m * 16, m * 16 + 16)
            left, right = h2_ref[n, tile].astype(F32), h2_ref[8 + n, tile].astype(F32)
            t_ref[pl.ds(2 * m * 128 + n, 16, stride=8), :] = jnp.where(lane16 < 64, left, right)
            if m < 2:
                t_ref[pl.ds((2 * m + 1) * 128 + n, 16, stride=8), :] = pltpu.roll(jnp.where(lane16 < 64, right, left), 64, 1)
    for r in range(8):
        for pair in range(STEPS // 2):
            parts = [t_ref[(2 * pair + j) * 64 + r * 8 : (2 * pair + j) * 64 + r * 8 + 8, :] for j in range(2)]
            g_ref[z, c, r, pair * 16 : pair * 16 + 16] = jnp.concatenate(parts, axis=0).astype(BF16)

    quarters = (yh, 2, 3)
    ag, ay, ac = {}, {}, []

    def piece(zz, half, index):
        return g_ref.at[zz, half, pl.ds(2 * index, 2)]

    def source(way, k):
        return zmod(-1 - k if way == 0 else 1 + k)

    def arrives(way, k, i):
        return k < 3 or (way == 0 and i < 2) or (way == 1 and i == 2)

    def pass_on(way, k, i):
        zz = z if k == 0 else source(way, k - 1)
        part = piece(zz, c, quarters[i])
        copy = rdma(part, part, ag_send.at[way, k, i], ag_recv.at[way, k, i], dev(z + 1 - 2 * way, yh, c, g))
        copy.start()
        ag[(way, k, i)] = copy

    def to_core(part, other, index, k):
        copy = rdma(part, part, ac_send.at[index], ac_recv.at[index], partner)
        copy.start()
        ac.append((copy, rdma(other, other, ac_send.at[index], ac_recv.at[index], partner), k))

    def arrived(way, k, i):
        ag[(way, k, i)].wait_recv()
        zz = source(way, k)
        part = piece(zz, c, quarters[i])
        if i == 0:
            other = piece(zz, c, 1 - yh)
            copy = rdma(part, part, ay_send.at[way, k], ay_recv.at[way, k], dev(z, 1 - yh, c, g))
            copy.start()
            ay[(way, k)] = (copy, rdma(other, other, ay_send.at[way, k], ay_recv.at[way, k], dev(z, 1 - yh, c, g)))
            if k == 3:
                copy = rdma(part, part, ay_send.at[1, 3], ay_recv.at[1, 3], dev(z, 1 - yh, 1 - c, g))
                copy.start()
                other = piece(zz, 1 - c, 1 - yh)
                ay[(1, 3)] = (copy, rdma(other, other, ay_send.at[1, 3], ay_recv.at[1, 3], partner))
        to_core(part, piece(zz, 1 - c, quarters[i]), (way * 4 + k) * 3 + i, k)

    def crossed(way, k):
        ay[(way, k)][1].wait_recv()
        zz = source(way, k)
        to_core(piece(zz, c, 1 - yh), piece(zz, 1 - c, 1 - yh), 24 + way * 4 + k, k)

    for i in range(3):
        for way in range(2):
            pass_on(way, 0, i)
    own_part, own_other = g_ref.at[z, c], g_ref.at[z, 1 - c]
    own_copy = rdma(own_part, own_part, ac_send.at[32], ac_recv.at[32], partner)
    own_copy.start()

    def final_arrived(k, carry):
        @pl.when(k != trial)
        def _():
            rdma(ffs_ref.at[pl.ds(0, 8)], ffr_ref.at[k], f_send.at[0], f_recv.at[k], partner).wait_recv()

        return carry

    lax.fori_loop(0, 16, final_arrived, 0)
    for k in range(16):
        value = pltpu.roll(ffr_ref[k], lax.rem(128 - 32 * q, 128), 1)
        ff_ref[k] = value[:, :32]

    for k in range(1, 4):
        for i in range(3):
            for way in range(2):
                if arrives(way, k, i):
                    arrived(way, k - 1, i)
                    pass_on(way, k, i)
        for i in range(3):
            for way in range(2):
                if not arrives(way, k, i):
                    arrived(way, k - 1, i)
        if k >= 2:
            for way in range(2):
                crossed(way, k - 2)

    near_planes = (z, zmod(1), zmod(-1), zmod(2), zmod(-2))
    far_planes = (zmod(3), zmod(-3), zmod(4))

    def product(region, planes):
        history = jnp.concatenate(
            [jnp.concatenate([g_ref[plane, 0, region], g_ref[plane, 1, region]], axis=0) for plane in planes], axis=1
        )
        band = jnp.concatenate(
            [band_ref[region, pl.ds(pl.multiple_of(plane * LANES, LANES), LANES), :] for plane in planes], axis=0
        )
        return jnp.dot(history, band, preferred_element_type=F32)

    def collect_near(region, carry):
        drive_ref[region] = product(region, near_planes)
        return carry

    rdma(own_other, own_other, ac_send.at[32], ac_recv.at[32], partner).wait_recv()
    for _, other, k in ac:
        if k < 2:
            other.wait_recv()
    lax.fori_loop(0, 4, collect_near, 0)
    crossed(0, 2)
    crossed(1, 2)
    for i in range(3):
        for way in range(2):
            if arrives(way, 3, i):
                arrived(way, 3, i)
    lax.fori_loop(4, 8, collect_near, 0)
    ay[(0, 3)][1].wait_recv()
    ay[(1, 3)][1].wait_recv()
    for _, other, k in ac:
        if k >= 2:
            other.wait_recv()

    slot8 = s * slots + lax.broadcasted_iota(jnp.int32, (8, slots), 1)

    def collect(region, carry):
        drive_ref[region] = drive_ref[region] + product(region, far_planes)
        live = slot8 < live_ref[region]
        for half in range(2):
            bins = trials_of(tbins_ref, half, region)
            voltage = trials_of(tstart_ref, half, region)
            for step in range(STEPS):
                start = half * ROWS + step * 8
                voltage = 0.9 * voltage + (0.5 * SCALE) * drive_ref[region, start : start + 8, :]
                voltage = jnp.where(bins == step, -0.5, voltage)
            voltage = jnp.where(live, voltage, 0.0)
            for tile in range(8):
                tstart_ref[pl.ds(tile * 128 + half * 64 + region, 8, stride=8), :] = voltage[:, tile * LANES : tile * LANES + LANES]
        return carry

    lax.fori_loop(0, 8, collect, 0)
    for tile in range(8):
        out_ref[:, tile * LANES : tile * LANES + LANES] = tstart_ref[tile * 128 : tile * 128 + 128, :]

    for copy in cx.values():
        copy.wait_send()
    for _, copy in quad:
        copy.wait_send()
    for copy in ring.values():
        copy.wait_send()
    lax.fori_loop(1, 8, sent_all(setup_own), 0)
    for copy in near:
        copy.wait_send()
    lax.fori_loop(1, 16, sent_all(trial_own), 0)
    lax.fori_loop(0, 16, sent_all(trial_near), 0)
    lax.fori_loop(1, 16, sent_all(back), 0)
    lax.fori_loop(1, 16, sent_all(final), 0)
    own_copy.wait_send()
    for copy in ag.values():
        copy.wait_send()
    for copy, _ in ay.values():
        copy.wait_send()
    for copy, _, _ in ac:
        copy.wait_send()


def local(spike_bins, neuron_site, efficacy, region_live, membrane_init, field_init, rim_weights, rim_codes):
    trials, regions, slots = spike_bins.shape
    rows = trials * regions
    vmem = pl.BlockSpec(memory_space=pltpu.VMEM)
    dma = pltpu.SemaphoreType.DMA
    field_final, membranes = pl.pallas_call(
        fused_kernel,
        out_shape=(jax.ShapeDtypeStruct((trials, regions, 32), F32), jax.ShapeDtypeStruct((rows, slots), F32)),
        in_specs=[pl.BlockSpec(memory_space=pltpu.SMEM)] + [vmem] * 7,
        out_specs=(vmem, vmem),
        scratch_shapes=[
            pltpu.VMEM((regions, slots), F32),
            pltpu.VMEM((1024, LANES), jnp.int32),
            pltpu.VMEM((1024, LANES), F32),
            pltpu.VMEM((8, 1024, slots), BF16),
            pltpu.VMEM((160, slots), BF16),
            pltpu.VMEM((8, 160, slots), F32),
            pltpu.VMEM((8, 2, 8, ROWS, LANES), BF16),
            pltpu.VMEM((8, 2, 8, ROWS, LANES), BF16),
            pltpu.VMEM((12, 8, LANES), F32),
            pltpu.VMEM((16, 8, LANES), F32),
            pltpu.VMEM((8, 8, ROWS, LANES), BF16),
            pltpu.VMEM((2, 4, 4, 2, ROWS, LANES), BF16),
            pltpu.VMEM((2, 4, 4, 2, ROWS, LANES), BF16),
            pltpu.VMEM((4, 12, 8, LANES), F32),
            pltpu.VMEM((4, 8, 8, LANES), F32),
            pltpu.VMEM((12, 8, LANES), F32),
            pltpu.VMEM((8, 8, LANES), F32),
            pltpu.VMEM((12, 8, LANES), F32),
            pltpu.VMEM((8, 8, LANES), F32),
            pltpu.VMEM((12, 8, LANES), F32),
            pltpu.VMEM((8, 8, LANES), F32),
            pltpu.VMEM((8, 12, 8, LANES), F32),
            pltpu.VMEM((8, 8, LANES), F32),
            pltpu.VMEM((640, LANES), F32),
            pltpu.VMEM((8, ROWS, LANES), BF16),
            pltpu.VMEM((2, 8, 32, LANES), BF16),
            pltpu.VMEM((16, ROWS, LANES), BF16),
            pltpu.VMEM((16, 32, LANES), BF16),
            pltpu.VMEM((STEPS, 64, LANES), F32),
            pltpu.VMEM((25, 64, LANES), F32),
            pltpu.VMEM((STEPS, 64, LANES), F32),
            pltpu.VMEM((8, 48, LANES), BF16),
            pltpu.VMEM((16, 48, LANES), BF16),
            pltpu.VMEM((640, LANES), F32),
            pltpu.VMEM((64, LANES), F32),
            pltpu.VMEM((16, 8, LANES), F32),
            dma((4,)), dma((4,)), dma((2, 4, 4)), dma((2, 4, 4)), dma((8,)), dma((8,)),
            dma((2,)), dma((2,)), dma((2, 8)), dma((2, 8)), dma((2, 16)), dma((2, 16)), dma((16,)), dma((16,)),
            dma((16,)), dma((16,)), dma((2, 4, 3)), dma((2, 4, 3)), dma((2, 4)), dma((2, 4)), dma((33,)), dma((33,)),
        ],
        compiler_params=pltpu.CompilerParams(vmem_limit_bytes=VMEM_LIMIT, collective_id=0, has_side_effects=True),
        name="window",
    )(
        region_live, spike_bins.reshape(rows, slots), neuron_site, efficacy,
        membrane_init.reshape(rows, slots), field_init, rim_weights, rim_codes,
    )
    return field_final, membranes.reshape(trials, regions, slots)


def solution(mesh):
    in_specs = (
        P(None, "neur", "surf"),
        P("neur", "surf"),
        P("neur", "surf"),
        P("neur"),
        P(None, "neur", "surf"),
        P(None, "neur", "surf"),
        P(None, "neur", "surf"),
        P(None, "neur", "surf"),
    )
    out_specs = (P(None, "neur", "surf"), P(None, "neur", "surf"))
    return jax.shard_map(local, mesh=mesh, in_specs=in_specs, out_specs=out_specs, check_vma=False)
```

time: 110 us -> 89.3 us (0.81)
  Pallas kernels: 99.4 us -> 85.1 us
  local copies, waits for them, and re-layouts: 8.13 us -> 3.36 us
  other arithmetic: 1.35 us -> 0 us
    pallas_call x3 -> x1, Pallas kernels: 99.4 us -> 85.1 us  [local(): pl.pallas_call(fused_kernel, out_shape=(jax.ShapeDtypeStruct((trials, reg...]
    reshape x2 -> x0, local copies, waits for them, and re-layouts: 3.91 us -> none  [the longest x1 2.48 us: local(): bins5 = spike_bins.reshape(2, 8, regions, 1, slots)]
    another operation x4 -> x0, local copies, waits for them, and re-layouts: 1.65 us -> none  [the longest x2 0.85 us: local(): init = jnp.tile(field_init, (1, 1, 4))]
    convert_element_type x2 -> x0, other arithmetic: 1.34 us -> none  [the longest x1 1.33 us: local(): efficacy.astype(F32)]
    unnamed x12 -> x2, local copies, waits for them, and re-layouts: 2.58 us -> 3.36 us
where the time goes in v2:
time: 89.3 us; the launch traced here: 89.1 us
  Pallas kernels  85.1 us (95%)
  local copies, waits for them, and re-layouts  3.36 us (4%)
    pallas_call x1, Pallas kernels, local(): pl.pallas_call(fused_kernel, out_shape=(jax.ShapeDtypeStruct((trials, reg...  85.1 us
    unnamed x2, local copies, waits for them, and re-layouts  3.36 us

profile of v2, /device:TPU:1, one launch (start us, length us, event | category | flops | bytes accessed | tf_op | source)
XLA Modules:
  0.0 89.1 jit_solution(10347782265724650655)
XLA Ops:
  0.6 85.1 %window.1 = (f32[16,8,32]{2,1,0:T(8,128)}, f32[128,1024]{1,0:T(8,128)}) custom-call(s32[8]{0:T(128)} %live_ref.1, s32[128,1024]{1,0:T(8,128)} %bitcast.3, s32[8,1024]{1,0:T(8,128)} %site_ref.1, bf16[8,1024]{1,0:T(8,128)(2,1)} %eff_ref.1, f32[128,1024]{1,0:T(8,128)} %bitcast.4, f32[16,8,32]{2,1,0:T(8,128)} %field_ref.1, f32[6,8,32]{2,1,0:T(8,128)} %weights_ref.1, ...), custom_call_target="tpu_custom_call" | custom-call | tf_op jit(solution)/shard_map/window/pallas_call | solution.py:607
  85.8 1.5 %copy.12 = f32[16,8,32]{2,1,0:T(8,128)} copy(f32[16,8,32]{2,1,0:T(8,128)} %get-tuple-element.8) | data formatting | bytes 32768
  87.3 1.9 %copy.13 = f32[16,8,1024]{2,1,0:T(8,128)} copy(f32[16,8,1024]{2,1,0:T(8,128)} %bitcast.5) | data formatting | bytes 1048576

commit v3 on v2

--- a/solution.py
+++ b/solution.py
@@ -46,7 +46,7 @@
     cx_ref, sbuf, rbuf, rq_ref, iq_ref, tl_ref, til_ref, th_ref, tih_ref, tm_ref, tim_ref, ro_ref, io_ref, p_ref, mb_ref, mh_ref,
     own_ref, hal_ref, inj_ref, cf_ref, hist_ref, mb2_ref, h2_ref, t_ref, ffs_ref, ffr_ref,
     cx_send, cx_recv, ring_send, ring_recv, q_send, q_recv, n_send, n_recv, r2_send, r2_recv, a_send, a_recv,
-    b_send, b_recv, f_send, f_recv, ag_send, ag_recv, ay_send, ay_recv, ac_send, ac_recv,
+    b_send, b_recv, f_send, f_recv, ag_send, ag_recv, ac_send, ac_recv,
 ):
     s = lax.axis_index("surf")
     g = lax.axis_index("neur")
@@ -103,7 +103,7 @@
         first = half * 64 + region
         return jnp.concatenate([ref[pl.ds(tile * 128 + first, 8, stride=8), :] for tile in range(8)], axis=1)
 
-    def spread(region, carry):
+    def spread(region, lot):
         weight = jnp.where(slot_id < live_ref[region], weff_ref[pl.ds(region, 1), :], 0.0)
         weight = jnp.broadcast_to(weight, (8, slots))
         band = band_ref.at[region]
@@ -113,19 +113,19 @@
             for pair in range(STEPS // 2):
                 rows = [jnp.where(bins == 2 * pair + j, weight, 0.0) for j in range(2)]
                 start = half * ROWS + pair * 16
-                charge_ref[start : start + 16, :] = jnp.concatenate(rows, axis=0).astype(BF16)
-        total = lax.dot_general(charge_ref[...], band[...], (((1,), (1,)), ((), ())), preferred_element_type=F32)
+                charge_ref[lot, start : start + 16, :] = jnp.concatenate(rows, axis=0).astype(BF16)
+        total = lax.dot_general(charge_ref[lot], band[...], (((1,), (1,)), ((), ())), preferred_element_type=F32)
         total = (total * SCALE).astype(BF16)
         for plane in range(8):
             for half in range(2):
                 s_ref[plane, half, region] = total[half * ROWS : half * ROWS + ROWS, plane * LANES : plane * LANES + LANES]
-        return carry
 
     partner = dev(z, yh, 1 - c, g)
     cx = {}
 
     def quarter(index):
-        lax.fori_loop(2 * index, 2 * index + 2, spread, 0)
+        for lot in range(2):
+            spread(2 * index + lot, lot)
 
     def to_partner(index):
         part = pl.ds(2 * index, 2)
@@ -269,6 +269,11 @@
     hop(3, 1)
     hop(2, 2)
 
+    hop(1, 3)
+    hop(3, 2)
+    hop(2, 3)
+    hop(3, 3)
+
     def setup_arrived(i, carry):
         gg = gmod(i)
         rdma(tm_ref, ro_ref.at[gg], r2_send.at[0, i], r2_recv.at[0, gg], partner).wait_recv()
@@ -304,11 +309,6 @@
                 code = (a + RIM) * (2 * RIM + 1) + b
                 cf_ref[code] = pltpu.roll(cf_ref[code], a % 64, 0)
 
-    hop(1, 3)
-    hop(3, 2)
-    hop(2, 3)
-    hop(3, 3)
-
     for index in range(4):
         value = x_of(0, index)
         for way in range(2):
@@ -325,7 +325,19 @@
             block16 < 2, jnp.where(block16 == 0, tiles[0], tiles[1]), jnp.where(block16 == 2, tiles[2], tiles[3])
         )
 
-    for n in range(8):
+    slot = yh * 8 + g
+
+    def trial_own(k):
+        n = gmod(k % 8)
+        return (rdma(mb_ref.at[n], own_ref.at[slot], a_send.at[0, k], a_recv.at[0, slot], dev(z, lax.rem(yh + k // 8, 2), c, n)),)
+
+    def trial_near(k):
+        n = gmod(k % 8)
+        up = k // 8
+        return (rdma(mh_ref.at[up, n], hal_ref.at[slot], a_send.at[1, k], a_recv.at[1, slot], dev(z + 1 - 2 * up, up, c, n)),)
+
+    def trial_send(i, carry):
+        n = gmod(i)
         tiles = []
         for pair in range(STEPS // 2):
             parts = [p_ref[pl.ds((2 * pair + j) * 8 + n, 8, stride=ROWS), :] for j in range(2)]
@@ -337,19 +349,18 @@
         mh_ref[1, n, :16] = by_block(low).astype(BF16)
         mh_ref[0, n, 16:] = tiles[4].astype(BF16)
         mh_ref[1, n, 16:] = tiles[4].astype(BF16)
-    slot = yh * 8 + g
-
-    def trial_own(k):
-        n = gmod(k % 8)
-        return (rdma(mb_ref.at[n], own_ref.at[slot], a_send.at[0, k], a_recv.at[0, slot], dev(z, lax.rem(yh + k // 8, 2), c, n)),)
-
-    def trial_near(k):
-        n = gmod(k % 8)
-        up = k // 8
-        return (rdma(mh_ref.at[up, n], hal_ref.at[slot], a_send.at[1, k], a_recv.at[1, slot], dev(z + 1 - 2 * up, up, c, n)),)
-
-    lax.fori_loop(1, 16, start_all(trial_own), 0)
-    lax.fori_loop(0, 16, start_all(trial_near), 0)
+        trial_own(i + 8)[0].start()
+        trial_near(i)[0].start()
+        trial_near(i + 8)[0].start()
+
+        @pl.when(i > 0)
+        def _():
+            trial_own(i)[0].start()
+
+        return carry
+
+    lax.fori_loop(1, 8, trial_send, 0)
+    trial_send(0, 0)
     own_ref[slot] = mb_ref[g]
 
     def trial_arrived(k, carry):
@@ -395,7 +406,19 @@
 
     mine64 = (lane16 >= 64 * yh) & (lane16 < 64 + 64 * yh)
 
-    def pack(gg, carry):
+    trial = c * 8 + g
+
+    def back(k):
+        gg = gmod(k % 8)
+        return (rdma(mb2_ref.at[gg], h2_ref.at[slot], b_send.at[k], b_recv.at[slot], dev(z, lax.rem(yh + k // 8, 2), c, gg)),)
+
+    def final(k):
+        gg = gmod(k % 8)
+        rows = pl.ds(pl.multiple_of(gg * 8, 8), 8)
+        return (rdma(ffs_ref.at[rows], ffr_ref.at[trial], f_send.at[k], f_recv.at[trial], dev(z, yh, lax.rem(c + k // 8, 2), gg)),)
+
+    def pack(i, carry):
+        gg = gmod(i)
         rows = pl.ds(pl.multiple_of(gg * 8, 8), 8)
         tiles = [
             jnp.concatenate([hist_ref[2 * pair, rows], hist_ref[2 * pair + 1, rows]], axis=0) for pair in range(STEPS // 2)
@@ -404,22 +427,16 @@
             both = jnp.where(mine64, tiles[2 * m], pltpu.roll(tiles[2 * m + 1], 64, 1))
             mb2_ref[gg, m * 16 : m * 16 + 16] = both.astype(BF16)
         mb2_ref[gg, 32:48] = tiles[4].astype(BF16)
-        return carry
-
-    lax.fori_loop(0, 8, pack, 0)
-
-    def back(k):
-        gg = gmod(k % 8)
-        return (rdma(mb2_ref.at[gg], h2_ref.at[slot], b_send.at[k], b_recv.at[slot], dev(z, lax.rem(yh + k // 8, 2), c, gg)),)
-
-    trial = c * 8 + g
-
-    def final(k):
-        gg = gmod(k % 8)
-        rows = pl.ds(pl.multiple_of(gg * 8, 8), 8)
-        return (rdma(ffs_ref.at[rows], ffr_ref.at[trial], f_send.at[k], f_recv.at[trial], dev(z, yh, lax.rem(c + k // 8, 2), gg)),)
-
-    lax.fori_loop(1, 16, start_all(back), 0)
+        back(i + 8)[0].start()
+
+        @pl.when(i > 0)
+        def _():
+            back(i)[0].start()
+
+        return carry
+
+    lax.fori_loop(1, 8, pack, 0)
+    pack(0, 0)
     lax.fori_loop(1, 16, start_all(final), 0)
     h2_ref[slot] = mb2_ref[g]
     ffr_ref[trial] = ffs_ref[pl.ds(pl.multiple_of(g * 8, 8), 8)]
@@ -444,8 +461,8 @@
             parts = [t_ref[(2 * pair + j) * 64 + r * 8 : (2 * pair + j) * 64 + r * 8 + 8, :] for j in range(2)]
             g_ref[z, c, r, pair * 16 : pair * 16 + 16] = jnp.concatenate(parts, axis=0).astype(BF16)
 
-    quarters = (yh, 2, 3)
-    ag, ay, ac = {}, {}, []
+    quarters = (0, 1, 2, 3)
+    ag, ac = {}, []
 
     def piece(zz, half, index):
         return g_ref.at[zz, half, pl.ds(2 * index, 2)]
@@ -454,7 +471,7 @@
         return zmod(-1 - k if way == 0 else 1 + k)
 
     def arrives(way, k, i):
-        return k < 3 or (way == 0 and i < 2) or (way == 1 and i == 2)
+        return k < 3 or (way == 0 and i < 2) or (way == 1 and i >= 2)
 
     def pass_on(way, k, i):
         zz = z if k == 0 else source(way, k - 1)
@@ -468,28 +485,12 @@
         copy.start()
         ac.append((copy, rdma(other, other, ac_send.at[index], ac_recv.at[index], partner), k))
 
-    def arrived(way, k, i):
-        ag[(way, k, i)].wait_recv()
+    def share(way, k, i):
         zz = source(way, k)
         part = piece(zz, c, quarters[i])
-        if i == 0:
-            other = piece(zz, c, 1 - yh)
-            copy = rdma(part, part, ay_send.at[way, k], ay_recv.at[way, k], dev(z, 1 - yh, c, g))
-            copy.start()
-            ay[(way, k)] = (copy, rdma(other, other, ay_send.at[way, k], ay_recv.at[way, k], dev(z, 1 - yh, c, g)))
-            if k == 3:
-                copy = rdma(part, part, ay_send.at[1, 3], ay_recv.at[1, 3], dev(z, 1 - yh, 1 - c, g))
-                copy.start()
-                other = piece(zz, 1 - c, 1 - yh)
-                ay[(1, 3)] = (copy, rdma(other, other, ay_send.at[1, 3], ay_recv.at[1, 3], partner))
-        to_core(part, piece(zz, 1 - c, quarters[i]), (way * 4 + k) * 3 + i, k)
-
-    def crossed(way, k):
-        ay[(way, k)][1].wait_recv()
-        zz = source(way, k)
-        to_core(piece(zz, c, 1 - yh), piece(zz, 1 - c, 1 - yh), 24 + way * 4 + k, k)
-
-    for i in range(3):
+        to_core(part, piece(zz, 1 - c, quarters[i]), (way * 4 + k) * 4 + i, k)
+
+    for i in range(4):
         for way in range(2):
             pass_on(way, 0, i)
     own_part, own_other = g_ref.at[z, c], g_ref.at[z, 1 - c]
@@ -509,18 +510,17 @@
         ff_ref[k] = value[:, :32]
 
     for k in range(1, 4):
-        for i in range(3):
+        for i in range(4):
             for way in range(2):
                 if arrives(way, k, i):
-                    arrived(way, k - 1, i)
+                    ag[(way, k - 1, i)].wait_recv()
                     pass_on(way, k, i)
-        for i in range(3):
+                    share(way, k - 1, i)
+        for i in range(4):
             for way in range(2):
                 if not arrives(way, k, i):
-                    arrived(way, k - 1, i)
-        if k >= 2:
-            for way in range(2):
-                crossed(way, k - 2)
+                    ag[(way, k - 1, i)].wait_recv()
+                    share(way, k - 1, i)
 
     near_planes = (z, zmod(1), zmod(-1), zmod(2), zmod(-2))
     far_planes = (zmod(3), zmod(-3), zmod(4))
@@ -543,15 +543,12 @@
         if k < 2:
             other.wait_recv()
     lax.fori_loop(0, 4, collect_near, 0)
-    crossed(0, 2)
-    crossed(1, 2)
-    for i in range(3):
+    for i in range(4):
         for way in range(2):
             if arrives(way, 3, i):
-                arrived(way, 3, i)
+                ag[(way, 3, i)].wait_recv()
+                share(way, 3, i)
     lax.fori_loop(4, 8, collect_near, 0)
-    ay[(0, 3)][1].wait_recv()
-    ay[(1, 3)][1].wait_recv()
     for _, other, k in ac:
         if k >= 2:
             other.wait_recv()
@@ -593,8 +590,6 @@
     own_copy.wait_send()
     for copy in ag.values():
         copy.wait_send()
-    for copy, _ in ay.values():
-        copy.wait_send()
     for copy, _, _ in ac:
         copy.wait_send()
 
@@ -614,7 +609,7 @@
             pltpu.VMEM((1024, LANES), jnp.int32),
             pltpu.VMEM((1024, LANES), F32),
             pltpu.VMEM((8, 1024, slots), BF16),
-            pltpu.VMEM((160, slots), BF16),
+            pltpu.VMEM((2, 160, slots), BF16),
             pltpu.VMEM((8, 160, slots), F32),
             pltpu.VMEM((8, 2, 8, ROWS, LANES), BF16),
             pltpu.VMEM((8, 2, 8, ROWS, LANES), BF16),
@@ -648,7 +643,7 @@
             pltpu.VMEM((16, 8, LANES), F32),
             dma((4,)), dma((4,)), dma((2, 4, 4)), dma((2, 4, 4)), dma((8,)), dma((8,)),
             dma((2,)), dma((2,)), dma((2, 8)), dma((2, 8)), dma((2, 16)), dma((2, 16)), dma((16,)), dma((16,)),
-            dma((16,)), dma((16,)), dma((2, 4, 3)), dma((2, 4, 3)), dma((2, 4)), dma((2, 4)), dma((33,)), dma((33,)),
+            dma((16,)), dma((16,)), dma((2, 4, 4)), dma((2, 4, 4)), dma((33,)), dma((33,)),
         ],
         compiler_params=pltpu.CompilerParams(vmem_limit_bytes=VMEM_LIMIT, collective_id=0, has_side_effects=True),
         name="window",

time: 89.3 us -> 82.6 us (0.925)
  Pallas kernels: 85.1 us -> 78.4 us
    pallas_call x1, Pallas kernels: 85.1 us -> 78.4 us  [local(): pl.pallas_call(fused_kernel, out_shape=(jax.ShapeDtypeStruct((trials, reg...]
where the time goes in v3:
time: 82.6 us; the launch traced here: 82.4 us
  Pallas kernels  78.4 us (95%)
  local copies, waits for them, and re-layouts  3.36 us (4%)
    pallas_call x1, Pallas kernels, local(): pl.pallas_call(fused_kernel, out_shape=(jax.ShapeDtypeStruct((trials, reg...  78.4 us
    unnamed x2, local copies, waits for them, and re-layouts  3.36 us

profile of v3, /device:TPU:1, one launch (start us, length us, event | category | flops | bytes accessed | tf_op | source)
XLA Modules:
  0.0 82.4 jit_solution(16869123273830479761)
XLA Ops:
  0.6 78.4 %window.1 = (f32[16,8,32]{2,1,0:T(8,128)}, f32[128,1024]{1,0:T(8,128)}) custom-call(s32[8]{0:T(128)} %live_ref.1, s32[128,1024]{1,0:T(8,128)} %bitcast.3, s32[8,1024]{1,0:T(8,128)} %site_ref.1, bf16[8,1024]{1,0:T(8,128)(2,1)} %eff_ref.1, f32[128,1024]{1,0:T(8,128)} %bitcast.4, f32[16,8,32]{2,1,0:T(8,128)} %field_ref.1, f32[6,8,32]{2,1,0:T(8,128)} %weights_ref.1, ...), custom_call_target="tpu_custom_call" | custom-call | tf_op jit(solution)/shard_map/window/pallas_call | solution.py:602
  79.0 1.5 %copy.12 = f32[16,8,32]{2,1,0:T(8,128)} copy(f32[16,8,32]{2,1,0:T(8,128)} %get-tuple-element.8) | data formatting | bytes 32768
  80.5 1.9 %copy.13 = f32[16,8,1024]{2,1,0:T(8,128)} copy(f32[16,8,1024]{2,1,0:T(8,128)} %bitcast.5) | data formatting | bytes 1048576

commit v4 on v3

--- a/solution.py
+++ b/solution.py
@@ -70,25 +70,18 @@
         return lax.rem(g + i, 8)
 
     barrier = pltpu.get_barrier_semaphore()
-    me = (yh * 2 + c) * 8 + g
-
-    def greet_plane(i, carry):
-        other = lax.rem(me + i, 32)
-        pl.semaphore_signal(
-            barrier, inc=1, device_id=dev(z, other // 16, (other // 8) % 2, other % 8), device_id_type=pl.DeviceIdType.MESH
-        )
-        return carry
-
-    lax.fori_loop(1, 32, greet_plane, 0)
-
-    def greet_near(i, carry):
-        pl.semaphore_signal(
-            barrier, inc=1, device_id=dev(z + dzh, i // 8, c, i % 8), device_id_type=pl.DeviceIdType.MESH
-        )
-        return carry
-
-    lax.fori_loop(0, 16, greet_near, 0)
-    pl.semaphore_signal(barrier, inc=1, device_id=dev(z - dzh, yh, c, g), device_id_type=pl.DeviceIdType.MESH)
+
+    def greet(target):
+        pl.semaphore_signal(barrier, inc=1, device_id=target, device_id_type=pl.DeviceIdType.MESH)
+
+    greet(dev(z, yh, 1 - c, g))
+    greet(dev(z, 1 - yh, 1 - c, g))
+    greet(dev(z - dzh, yh, c, g))
+    for a in range(2):
+        for i in range(8):
+            if a or i:
+                greet(dev(z, lax.rem(yh + a, 2), c, gmod(i)))
+            greet(dev(z + dzh, a, c, i))
 
     slots = site_ref.shape[1]
     slot_id = s * slots + lax.broadcasted_iota(jnp.int32, (1, slots), 1)
@@ -133,7 +126,7 @@
         cx[index].start()
 
     quarter(0)
-    pl.semaphore_wait(barrier, 31 + 17)
+    pl.semaphore_wait(barrier, 2 + 15 + 17)
     to_partner(0)
 
     q = yh * 2 + c
@@ -415,7 +408,7 @@
     def final(k):
         gg = gmod(k % 8)
         rows = pl.ds(pl.multiple_of(gg * 8, 8), 8)
-        return (rdma(ffs_ref.at[rows], ffr_ref.at[trial], f_send.at[k], f_recv.at[trial], dev(z, yh, lax.rem(c + k // 8, 2), gg)),)
+        return (rdma(ffs_ref.at[rows], ffr_ref.at[trial], f_send.at[k], f_recv.at[trial], dev(z, yh, c, gg)),)
 
     def pack(i, carry):
         gg = gmod(i)
@@ -437,7 +430,7 @@
 
     lax.fori_loop(1, 8, pack, 0)
     pack(0, 0)
-    lax.fori_loop(1, 16, start_all(final), 0)
+    lax.fori_loop(1, 8, start_all(final), 0)
     h2_ref[slot] = mb2_ref[g]
     ffr_ref[trial] = ffs_ref[pl.ds(pl.multiple_of(g * 8, 8), 8)]
 
@@ -456,11 +449,6 @@
             t_ref[pl.ds(2 * m * 128 + n, 16, stride=8), :] = jnp.where(lane16 < 64, left, right)
             if m < 2:
                 t_ref[pl.ds((2 * m + 1) * 128 + n, 16, stride=8), :] = pltpu.roll(jnp.where(lane16 < 64, right, left), 64, 1)
-    for r in range(8):
-        for pair in range(STEPS // 2):
-            parts = [t_ref[(2 * pair + j) * 64 + r * 8 : (2 * pair + j) * 64 + r * 8 + 8, :] for j in range(2)]
-            g_ref[z, c, r, pair * 16 : pair * 16 + 16] = jnp.concatenate(parts, axis=0).astype(BF16)
-
     quarters = (0, 1, 2, 3)
     ag, ac = {}, []
 
@@ -490,25 +478,26 @@
         part = piece(zz, c, quarters[i])
         to_core(part, piece(zz, 1 - c, quarters[i]), (way * 4 + k) * 4 + i, k)
 
-    for i in range(4):
-        for way in range(2):
-            pass_on(way, 0, i)
+    for r in range(8):
+        for pair in range(STEPS // 2):
+            parts = [t_ref[(2 * pair + j) * 64 + r * 8 : (2 * pair + j) * 64 + r * 8 + 8, :] for j in range(2)]
+            g_ref[z, c, r, pair * 16 : pair * 16 + 16] = jnp.concatenate(parts, axis=0).astype(BF16)
+        if r % 2 == 1:
+            for way in range(2):
+                pass_on(way, 0, r // 2)
     own_part, own_other = g_ref.at[z, c], g_ref.at[z, 1 - c]
     own_copy = rdma(own_part, own_part, ac_send.at[32], ac_recv.at[32], partner)
     own_copy.start()
 
-    def final_arrived(k, carry):
-        @pl.when(k != trial)
-        def _():
-            rdma(ffs_ref.at[pl.ds(0, 8)], ffr_ref.at[k], f_send.at[0], f_recv.at[k], partner).wait_recv()
-
-        return carry
-
-    lax.fori_loop(0, 16, final_arrived, 0)
-    for k in range(16):
-        value = pltpu.roll(ffr_ref[k], lax.rem(128 - 32 * q, 128), 1)
-        ff_ref[k] = value[:, :32]
-
+    def final_arrived(i, carry):
+        k = c * 8 + gmod(i)
+        rdma(ffs_ref.at[pl.ds(0, 8)], ffr_ref.at[k], f_send.at[0], f_recv.at[k], partner).wait_recv()
+        return carry
+
+    lax.fori_loop(1, 8, final_arrived, 0)
+    core_trials = ffr_ref.at[pl.ds(c * 8, 8)]
+    finals = rdma(core_trials, core_trials, f_send.at[8], f_recv.at[16], partner)
+    finals.start()
     for k in range(1, 4):
         for i in range(4):
             for way in range(2):
@@ -523,7 +512,8 @@
                     share(way, k - 1, i)
 
     near_planes = (z, zmod(1), zmod(-1), zmod(2), zmod(-2))
-    far_planes = (zmod(3), zmod(-3), zmod(4))
+    third_planes = (zmod(3), zmod(-3))
+    far_planes = (zmod(4),)
 
     def product(region, planes):
         history = jnp.concatenate(
@@ -538,20 +528,33 @@
         drive_ref[region] = product(region, near_planes)
         return carry
 
+    def collect_third(region, carry):
+        drive_ref[region] = drive_ref[region] + product(region, third_planes)
+        return carry
+
+    def from_core(first, last):
+        for _, other, k in ac:
+            if first <= k <= last:
+                other.wait_recv()
+
     rdma(own_other, own_other, ac_send.at[32], ac_recv.at[32], partner).wait_recv()
-    for _, other, k in ac:
-        if k < 2:
-            other.wait_recv()
-    lax.fori_loop(0, 4, collect_near, 0)
+    from_core(0, 1)
+    lax.fori_loop(0, 6, collect_near, 0)
     for i in range(4):
         for way in range(2):
             if arrives(way, 3, i):
                 ag[(way, 3, i)].wait_recv()
                 share(way, 3, i)
-    lax.fori_loop(4, 8, collect_near, 0)
-    for _, other, k in ac:
-        if k >= 2:
-            other.wait_recv()
+    lax.fori_loop(6, 8, collect_near, 0)
+    from_core(2, 2)
+    lax.fori_loop(0, 8, collect_third, 0)
+    other_trials = ffr_ref.at[pl.ds((1 - c) * 8, 8)]
+    rdma(other_trials, other_trials, f_send.at[8], f_recv.at[16], partner).wait_recv()
+    for k in range(16):
+        value = pltpu.roll(ffr_ref[k], lax.rem(128 - 32 * q, 128), 1)
+        ff_ref[k] = value[:, :32]
+
+    from_core(3, 3)
 
     slot8 = s * slots + lax.broadcasted_iota(jnp.int32, (8, slots), 1)
 
@@ -586,7 +589,8 @@
     lax.fori_loop(1, 16, sent_all(trial_own), 0)
     lax.fori_loop(0, 16, sent_all(trial_near), 0)
     lax.fori_loop(1, 16, sent_all(back), 0)
-    lax.fori_loop(1, 16, sent_all(final), 0)
+    lax.fori_loop(1, 8, sent_all(final), 0)
+    finals.wait_send()
     own_copy.wait_send()
     for copy in ag.values():
         copy.wait_send()
@@ -643,7 +647,7 @@
             pltpu.VMEM((16, 8, LANES), F32),
             dma((4,)), dma((4,)), dma((2, 4, 4)), dma((2, 4, 4)), dma((8,)), dma((8,)),
             dma((2,)), dma((2,)), dma((2, 8)), dma((2, 8)), dma((2, 16)), dma((2, 16)), dma((16,)), dma((16,)),
-            dma((16,)), dma((16,)), dma((2, 4, 4)), dma((2, 4, 4)), dma((33,)), dma((33,)),
+            dma((16,)), dma((17,)), dma((2, 4, 4)), dma((2, 4, 4)), dma((33,)), dma((33,)),
         ],
         compiler_params=pltpu.CompilerParams(vmem_limit_bytes=VMEM_LIMIT, collective_id=0, has_side_effects=True),
         name="window",

time: 82.6 us -> 81.6 us (0.988)
  Pallas kernels: 78.4 us -> 77.3 us
    pallas_call x1, Pallas kernels: 78.4 us -> 77.3 us  [local(): pl.pallas_call(fused_kernel, out_shape=(jax.ShapeDtypeStruct((trials, reg...]
where the time goes in v4:
time: 81.6 us; the launch traced here: 81.3 us
  Pallas kernels  77.3 us (95%)
  local copies, waits for them, and re-layouts  3.36 us (4%)
    pallas_call x1, Pallas kernels, local(): pl.pallas_call(fused_kernel, out_shape=(jax.ShapeDtypeStruct((trials, reg...  77.3 us
    unnamed x2, local copies, waits for them, and re-layouts  3.36 us

profile of v4, /device:TPU:1, one launch (start us, length us, event | category | flops | bytes accessed | tf_op | source)
XLA Modules:
  0.0 81.3 jit_solution(15917695320397782781)
XLA Ops:
  0.6 77.3 %window.1 = (f32[16,8,32]{2,1,0:T(8,128)}, f32[128,1024]{1,0:T(8,128)}) custom-call(s32[8]{0:T(128)} %live_ref.1, s32[128,1024]{1,0:T(8,128)} %bitcast.3, s32[8,1024]{1,0:T(8,128)} %site_ref.1, bf16[8,1024]{1,0:T(8,128)(2,1)} %eff_ref.1, f32[128,1024]{1,0:T(8,128)} %bitcast.4, f32[16,8,32]{2,1,0:T(8,128)} %field_ref.1, f32[6,8,32]{2,1,0:T(8,128)} %weights_ref.1, ...), custom_call_target="tpu_custom_call" | custom-call | tf_op jit(solution)/shard_map/window/pallas_call | solution.py:606
  77.9 1.5 %copy.12 = f32[16,8,32]{2,1,0:T(8,128)} copy(f32[16,8,32]{2,1,0:T(8,128)} %get-tuple-element.8) | data formatting | bytes 32768
  79.4 1.9 %copy.13 = f32[16,8,1024]{2,1,0:T(8,128)} copy(f32[16,8,1024]{2,1,0:T(8,128)} %bitcast.5) | data formatting | bytes 1048576

commit v5 on v4

--- a/solution.py
+++ b/solution.py
@@ -128,25 +128,6 @@
     quarter(0)
     pl.semaphore_wait(barrier, 2 + 15 + 17)
     to_partner(0)
-
-    q = yh * 2 + c
-    for k in range(6):
-        rim_ref[k] = jnp.concatenate([weights_ref[k]] * 4, axis=1)
-        rim_ref[6 + k] = jnp.concatenate([codes_ref[k].astype(F32)] * 4, axis=1)
-    for k in range(16):
-        init_ref[k] = jnp.concatenate([field_ref[k]] * 4, axis=1)
-    quad = []
-    for i in range(1, 4):
-        y2 = lax.rem(yh + i // 2, 2)
-        c2 = lax.rem(c + i % 2, 2)
-        target = dev(z, y2, c2, g)
-        quad.append((y2 * 2 + c2, rdma(rim_ref, rq_ref.at[q], q_send.at[i], q_recv.at[q], target)))
-        quad.append((y2 * 2 + c2, rdma(init_ref.at[pl.ds(c2 * 8, 8)], iq_ref.at[q], q_send.at[4 + i], q_recv.at[4 + q], target)))
-    for _, copy in quad:
-        copy.start()
-    rq_ref[q] = rim_ref[...]
-    iq_ref[q] = init_ref[pl.ds(c * 8, 8)]
-
 
     def x_of(dz, index):
         zd = zmod(dz)
@@ -178,6 +159,25 @@
     to_partner(1)
     cx[0].wait_recv()
     hop(0, 0)
+    q = yh * 2 + c
+    for k in range(6):
+        rim_ref[k] = jnp.concatenate([weights_ref[k]] * 4, axis=1)
+        rim_ref[6 + k] = jnp.concatenate([codes_ref[k].astype(F32)] * 4, axis=1)
+    for k in range(16):
+        init_ref[k] = jnp.concatenate([field_ref[k]] * 4, axis=1)
+    quad = []
+    for i in range(1, 4):
+        y2 = lax.rem(yh + i // 2, 2)
+        c2 = lax.rem(c + i % 2, 2)
+        target = dev(z, y2, c2, g)
+        quad.append((y2 * 2 + c2, rdma(rim_ref, rq_ref.at[q], q_send.at[i], q_recv.at[q], target)))
+        quad.append((y2 * 2 + c2, rdma(init_ref.at[pl.ds(c2 * 8, 8)], iq_ref.at[q], q_send.at[4 + i], q_recv.at[4 + q], target)))
+    for _, copy in quad:
+        copy.start()
+    rq_ref[q] = rim_ref[...]
+    iq_ref[q] = init_ref[pl.ds(c * 8, 8)]
+
+
     quarter(2)
     to_partner(2)
     cx[1].wait_recv()

time: 81.6 us -> 81.4 us (level)
  no operation moved by 1% of the time
where the time goes in v5:
time: 81.4 us; the launch traced here: 80.8 us
  Pallas kernels  76.8 us (94%)
  local copies, waits for them, and re-layouts  3.36 us (4%)
    pallas_call x1, Pallas kernels, local(): pl.pallas_call(fused_kernel, out_shape=(jax.ShapeDtypeStruct((trials, reg...  76.8 us
    unnamed x2, local copies, waits for them, and re-layouts  3.36 us

profile of v5, /device:TPU:1, one launch (start us, length us, event | category | flops | bytes accessed | tf_op | source)
XLA Modules:
  0.0 80.8 jit_solution(2184317616889287923)
XLA Ops:
  0.6 76.8 %window.1 = (f32[16,8,32]{2,1,0:T(8,128)}, f32[128,1024]{1,0:T(8,128)}) custom-call(s32[8]{0:T(128)} %live_ref.1, s32[128,1024]{1,0:T(8,128)} %bitcast.3, s32[8,1024]{1,0:T(8,128)} %site_ref.1, bf16[8,1024]{1,0:T(8,128)(2,1)} %eff_ref.1, f32[128,1024]{1,0:T(8,128)} %bitcast.4, f32[16,8,32]{2,1,0:T(8,128)} %field_ref.1, f32[6,8,32]{2,1,0:T(8,128)} %weights_ref.1, ...), custom_call_target="tpu_custom_call" | custom-call | tf_op jit(solution)/shard_map/window/pallas_call | solution.py:606
  77.4 1.5 %copy.12 = f32[16,8,32]{2,1,0:T(8,128)} copy(f32[16,8,32]{2,1,0:T(8,128)} %get-tuple-element.8) | data formatting | bytes 32768
  78.9 1.9 %copy.13 = f32[16,8,1024]{2,1,0:T(8,128)} copy(f32[16,8,1024]{2,1,0:T(8,128)} %bitcast.5) | data formatting | bytes 1048576
